TPU v7x, 512 devices: a whole 4x8x8 slice. The times are simulated.
512 devices in a mesh: grp: 8 (over z_hi, x), gx: 8 (over z_lo, core), gy: 8 (over y).
Axes of the slice: x: 4, y: 8, z: 8 (z_hi: 2, z_lo: 4; z = z_hi * 4 + z_lo), core: 2. Of those that a mesh axis runs over, the one named last changes fastest.
Arguments:
- efield: float32 [8, 3, 128, 128, 128], P('grp', None, 'gx', 'gy'), may hold values from -6 to 6
- hfield: float32 [8, 3, 128, 128, 128], P('grp', None, 'gx', 'gy'), may hold values from -6 to 6
- fwd_dft: bfloat16 [8, 2, 2, 3, 128, 128, 128], P('grp', None, None, None, 'gx', 'gy'), may hold values from -6 to 6
- adj_dft: bfloat16 [8, 2, 2, 3, 128, 128, 128], P('grp', None, None, None, 'gx', 'gy'), may hold values from -6 to 6
- permittivity: float32 [128, 128, 128], P('gx', 'gy'), may hold values from 1 to 4
- source_amp: float32 [8, 128, 128], P('grp', 'gx', 'gy'), may hold values from -6 to 6
- source_plane: int32 [8], P('grp'), may hold values from 4 to 123
- freqs: float32 [8, 2], P('grp'), may hold values from 0.2 to 1.5
- pml_width: int32 [2], replicated, may hold values from 2 to 7
- design_blocks: int32 [128], replicated, may hold values from 0 to 255, as said below
Outputs:
- grad_step: float32 [2, 128, 128, 128], P(None, 'gx', 'gy')
Inputs may be any that keep to these rules, and one draw needn't show every extreme that they name: `design_blocks`: distinct block numbers.
All inputs are finite; a program needn't handle non-finite values.
Results may differ from a plain program's by a relative error of at most 0.0003.
Values sent between devices are 32-bit elements; how exact they have to be, the bound alone decides.
A program may use at most 64 MiB of HBM per device.

v0:
```python
import jax
import jax.numpy as jnp
from jax import lax
from jax.sharding import PartitionSpec as P

BS = 8
STEPS = 2


courant = 0.5
absorb = 0.8


def shifted(value, axis, steps):
    count = lax.axis_size(axis)
    leading, last = (max(0, -steps), min(count, count - steps))
    return lax.ppermute(value, axis, [(source, source + steps) for source in range(leading, last)])


def ahead_z(field):
    zero = jnp.zeros_like(field[:, :, :1])
    return jnp.concatenate([field[:, :, 1:], zero], 2) - field


def behind_z(field):
    zero = jnp.zeros_like(field[:, :, :1])
    return field - jnp.concatenate([zero, field[:, :, :-1]], 2)


def profile(cells, count, width):
    place = cells.astype(jnp.float32)
    dist = jnp.minimum(place, count - 1.0 - place)
    wide = width.astype(jnp.float32)
    return jnp.maximum(0.0, (wide - dist) / wide) ** 2


def update_magnetic(fields_e, fields_h, damp):
    ex, ey, ez = fields_e
    hx, hy, hz = fields_h
    rim_x = shifted(jnp.stack([ey[0], ez[0]]), "gx", -1)
    rim_y = shifted(jnp.stack([ex[:, 0], ez[:, 0]]), "gy", -1)
    ey_dx = jnp.concatenate([ey[1:], rim_x[0][None]], 0) - ey
    ez_dx = jnp.concatenate([ez[1:], rim_x[1][None]], 0) - ez
    ex_dy = jnp.concatenate([ex[:, 1:], rim_y[0][:, None]], 1) - ex
    ez_dy = jnp.concatenate([ez[:, 1:], rim_y[1][:, None]], 1) - ez
    hx = damp * (hx - courant * (ez_dy - ahead_z(ey)))
    hy = damp * (hy - courant * (ahead_z(ex) - ez_dx))
    hz = damp * (hz - courant * (ey_dx - ex_dy))
    return (hx, hy, hz)


def update_electric(fields_e, fields_h, damp, coef, drive):
    ex, ey, ez = fields_e
    hx, hy, hz = fields_h
    last_x = hx.shape[0] - 1
    last_y = hx.shape[1] - 1
    rim_x = shifted(jnp.stack([hy[last_x], hz[last_x]]), "gx", 1)
    rim_y = shifted(jnp.stack([hx[:, last_y], hz[:, last_y]]), "gy", 1)
    hy_dx = hy - jnp.concatenate([rim_x[0][None], hy[:-1]], 0)
    hz_dx = hz - jnp.concatenate([rim_x[1][None], hz[:-1]], 0)
    hx_dy = hx - jnp.concatenate([rim_y[0][:, None], hx[:, :-1]], 1)
    hz_dy = hz - jnp.concatenate([rim_y[1][:, None], hz[:, :-1]], 1)
    ex = damp * (ex + coef * (hz_dy - behind_z(hy)))
    ey = damp * (ey + coef * (behind_z(hx) - hz_dx))
    ez = damp * (ez + coef * (hy_dx - hx_dy) + drive)
    return (ex, ey, ez)


def body(
    efield,
    hfield,
    fwd_dft,
    adj_dft,
    permittivity,
    source_amp,
    source_plane,
    freqs,
    pml_width,
    design_blocks,
):
    cells_x, cells_y, cells_z = permittivity.shape
    total_x = cells_x * lax.axis_size("gx")
    total_y = cells_y * lax.axis_size("gy")
    global_x = lax.axis_index("gx") * cells_x + jnp.arange(cells_x, dtype=jnp.int32)
    global_y = lax.axis_index("gy") * cells_y + jnp.arange(cells_y, dtype=jnp.int32)
    plane = (jnp.arange(cells_z, dtype=jnp.int32) == source_plane[0]).astype(jnp.float32)
    shaped = source_amp[0][:, :, None] * plane[None, None, :]
    omega = freqs[0]
    acc = adj_dft[0].astype(jnp.float32)
    damp = jnp.exp(
        -absorb
        * (
            profile(global_x, total_x, pml_width[0])[:, None]
            + profile(global_y, total_y, pml_width[1])[None, :]
        )
    )[:, :, None]
    coef = courant / permittivity
    fields_e = (efield[0, 0], efield[0, 1], efield[0, 2])
    fields_h = (hfield[0, 0], hfield[0, 1], hfield[0, 2])
    for step in range(STEPS):
        tval = jnp.float32(step + 1)
        fields_h = update_magnetic(fields_e, fields_h, damp)
        fields_e = update_electric(
            fields_e, fields_h, damp, coef, shaped * jnp.sin(omega[0] * tval)
        )
        efull = jnp.stack(fields_e)
        cosv = jnp.cos(omega * tval)[:, None, None, None, None]
        sinv = jnp.sin(omega * tval)[:, None, None, None, None]
        acc = jnp.stack([acc[:, 0] + cosv * efull, acc[:, 1] - sinv * efull], axis=1)
    cell_id = (global_x // BS)[:, None] * (total_y // BS) + (global_y // BS)[None, :]
    mask = jnp.any(design_blocks[:, None, None] == cell_id[None], axis=0).astype(jnp.float32)[
        :, :, None
    ]
    term = jnp.sum(fwd_dft[0].astype(jnp.float32) * acc, axis=(1, 2)) * mask[None]
    count = jnp.float32(design_blocks.shape[0] * BS * BS * cells_z)
    grad = lax.psum(term, "grp")
    squares = lax.psum(jnp.sum(grad * grad, axis=(1, 2, 3)), ("gx", "gy"))
    return grad / jnp.sqrt(squares / count + 1e-05)[:, None, None, None]


def solution(mesh):
    in_specs = (
        P("grp", None, "gx", "gy", None),
        P("grp", None, "gx", "gy", None),
        P("grp", None, None, None, "gx", "gy", None),
        P("grp", None, None, None, "gx", "gy", None),
        P("gx", "gy", None),
        P("grp", "gx", "gy"),
        P("grp"),
        P("grp", None),
        P(),
        P(),
    )
    out_specs = P(None, "gx", "gy", None)
    return jax.shard_map(body, mesh=mesh, in_specs=in_specs, out_specs=out_specs, check_vma=False)
```

profile of v0, /device:TPU:8, one launch (start us, length us, event | category | flops | bytes accessed | tf_op | source)
XLA Modules:
  0.0 310.4 jit_solution(465055666218704547)
XLA Ops:
  6.5 1.1 slice_bitcast_fusion.1
  7.7 7.7 %collective-permute-start.1 = (f32[2,16,128]{2,1,0:T(8,128)S(1)}, f32[2,16,128]{2,1,0:T(8,128)S(1)}, u32[]{:S(2)}, u32[]{:S(2)}) collective-permute-start(f32[2,16,128]{2,1,0:T(8,128)S(1)} %pad_maximum_fusion.3), channel_id=1, source_target_pairs={{1,0},{2,1},{3,2},{4,3},{5,4},{6,5},{7,6},{9,8},{10,9},{11,10},{12... | collective-permute-start | bytes 49160 | tf_op jit(solution)/shard_map/ppermute | solution.py:17
  15.5 0.7 slice_bitcast_fusion.6
  16.2 1.3 collective-permute-start
  17.5 1.0 slice_bitcast_fusion.4
  18.5 1.4 fusion.73
  21.9 0.7 cosine_bitcast_fusion.1
  23.0 0.4 compare_reduce_fusion
  24.3 3.0 collective-permute-start.3
  27.4 1.9 collective-permute-start.2
  29.4 3.7 %collective-permute-done.2 = f32[2,16,128]{2,1,0:T(8,128)S(1)} collective-permute-done((f32[2,16,128]{2,1,0:T(8,128)S(1)}, f32[2,16,128]{2,1,0:T(8,128)S(1)}, u32[]{:S(2)}, u32[]{:S(2)}) %collective-permute-start.2) | collective-permute-done | bytes 16416 | tf_op jit(solution)/shard_map/ppermute | solution.py:17
  33.5 1.3 collective-permute-start.4
  35.1 1.9 collective-permute-start.5
  37.0 3.7 %collective-permute-done.5 = f32[2,16,128]{2,1,0:T(8,128)S(1)} collective-permute-done((f32[2,16,128]{2,1,0:T(8,128)S(1)}, f32[2,16,128]{2,1,0:T(8,128)S(1)}, u32[]{:S(2)}, u32[]{:S(2)}) %collective-permute-start.5) | collective-permute-done | bytes 16416 | tf_op jit(solution)/shard_map/ppermute | solution.py:17
  41.0 2.0 collective-permute-start.7
  43.1 1.9 collective-permute-start.6
  45.2 3.6 %collective-permute-done.6 = f32[2,16,128]{2,1,0:T(8,128)S(1)} collective-permute-done((f32[2,16,128]{2,1,0:T(8,128)S(1)}, f32[2,16,128]{2,1,0:T(8,128)S(1)}, u32[]{:S(2)}, u32[]{:S(2)}) %collective-permute-start.6) | collective-permute-done | bytes 16416 | tf_op jit(solution)/shard_map/ppermute | solution.py:17
  49.0 0.3 fusion.2
  49.3 0.8 copy-done.3
  50.3 0.8 broadcast_multiply_fusion
  51.1 115.3 %all-reduce.10.cloned.1.call-done = f32[2,16,16,128]{3,2,1,0:T(8,128)} async-done(((f32[2,16,16,128]{3,2,1,0:T(8,128)}), f32[2,16,16,128]{3,2,1,0:T(8,128)}) %all-reduce.10.cloned.1.call-update) | async-done | bytes 262160 | tf_op jit(solution)/shard_map/psum | solution.py:116
  166.4 1.1 multiply_reduce_fusion
  167.5 134.2 %psum.15 = f32[2]{0:T(128)S(1)} all-reduce(f32[2]{0:T(128)S(1)} %multiply_reduce_fusion), channel_id=1, replica_groups=mesh['grp'=8,'gx'=8,'gy'=8] {'gx','gy'}, use_global_device_ids=true, to_apply=%region_4.5 | all-reduce | flops 2 | bytes 16 | tf_op jit(solution)/shard_map/psum | solution.py:117
  301.8 1.7 broadcast_divide_fusion
  (84 shorter events, 2.4 us)
Async XLA Ops:
  6.5 16.0 %copy-start.2 = (bf16[1,2,2,3,16,16,128]{6,5,4,3,2,1,0:T(8,128)(2,1)S(1)}, bf16[1,2,2,3,16,16,128]{6,5,4,3,2,1,0:T(8,128)(2,1)}, u32[]{:S(2)}) copy-start(bf16[1,2,2,3,16,16,128]{6,5,4,3,2,1,0:T(8,128)(2,1)} %param.13) | copy-start | bytes 2359300
  6.5 159.9 %all-reduce.10.cloned.1.call-start = ((), (), s32[]{:S(2)}) async-start(), calls=%async_computation | async-start | bytes 524288 | tf_op jit(solution)/shard_map/psum | solution.py:116
  7.7 15.3 %copy-start.7 = (s32[128]{0:T(128)S(1)}, s32[128]{0:T(128)}, u32[]{:S(2)}) copy-start(s32[128]{0:T(128)} %param.19) | copy-start | bytes 1540
  7.7 16.2 %collective-permute-start.1 = (f32[2,16,128]{2,1,0:T(8,128)S(1)}, f32[2,16,128]{2,1,0:T(8,128)S(1)}, u32[]{:S(2)}, u32[]{:S(2)}) collective-permute-start(f32[2,16,128]{2,1,0:T(8,128)S(1)} %pad_maximum_fusion.3), channel_id=1, source_target_pairs={{1,0},{2,1},{3,2},{4,3},{5,4},{6,5},{7,6},{9,8},{10,9},{11,10},{12... | collective-permute-start | bytes 49160 | tf_op jit(solution)/shard_map/ppermute | solution.py:17
  16.2 7.8 %collective-permute-start = (f32[2,16,128]{2,1,0:T(8,128)S(1)}, f32[2,16,128]{2,1,0:T(8,128)S(1)}, u32[]{:S(2)}, u32[]{:S(2)}) collective-permute-start(f32[2,16,128]{2,1,0:T(8,128)S(1)} %pad_maximum_fusion.2), channel_id=1, source_target_pairs={{8,0},{16,8},{24,16},{32,24},{40,32},{48,40},{56,48},{9,1},{17,9},... | collective-permute-start | bytes 49160 | tf_op jit(solution)/shard_map/ppermute | solution.py:17
  22.6 1.1 copy-start.6
  22.6 1.4 copy-start
  22.6 1.4 copy-start.4
  23.7 9.4 %copy-start.1 = (f32[16,16,128]{2,1,0:T(8,128)S(1)}, f32[16,16,128]{2,1,0:T(8,128)}, u32[]{:S(2)}) copy-start(f32[16,16,128]{2,1,0:T(8,128)} %param.14) | copy-start | bytes 393220
  23.7 9.4 %copy-start.5 = (f32[1,16,16]{2,1,0:T(8,128)S(1)}, f32[1,16,16]{2,1,0:T(8,128)}, u32[]{:S(2)}) copy-start(f32[1,16,16]{2,1,0:T(8,128)} %param.15) | copy-start | bytes 3076
  24.3 5.0 %collective-permute-start.3 = (f32[2,16,128]{2,1,0:T(8,128)S(1)}, f32[2,16,128]{2,1,0:T(8,128)S(1)}, u32[]{:S(2)}, u32[]{:S(2)}) collective-permute-start(f32[2,16,128]{2,1,0:T(8,128)S(1)} %pad_maximum_fusion.5), channel_id=1, source_target_pairs={{0,8},{8,16},{16,24},{24,32},{32,40},{40,48},{48,56},{1,9},{9,17},... | collective-permute-start | bytes 49160 | tf_op jit(solution)/shard_map/ppermute | solution.py:17
  27.4 5.6 %collective-permute-start.2 = (f32[2,16,128]{2,1,0:T(8,128)S(1)}, f32[2,16,128]{2,1,0:T(8,128)S(1)}, u32[]{:S(2)}, u32[]{:S(2)}) collective-permute-start(f32[2,16,128]{2,1,0:T(8,128)S(1)} %pad_maximum_fusion.4), channel_id=1, source_target_pairs={{0,1},{1,2},{2,3},{3,4},{4,5},{5,6},{6,7},{8,9},{9,10},{10,11},{11... | collective-permute-start | bytes 49160 | tf_op jit(solution)/shard_map/ppermute | solution.py:17
  33.5 3.6 %collective-permute-start.4 = (f32[2,16,128]{2,1,0:T(8,128)S(1)}, f32[2,16,128]{2,1,0:T(8,128)S(1)}, u32[]{:S(2)}, u32[]{:S(2)}) collective-permute-start(f32[2,16,128]{2,1,0:T(8,128)S(1)} %pad_maximum_fusion.6), channel_id=1, source_target_pairs={{8,0},{16,8},{24,16},{32,24},{40,32},{48,40},{56,48},{9,1},{17,9},... | collective-permute-start | bytes 49160 | tf_op jit(solution)/shard_map/ppermute | solution.py:17
  35.1 5.6 %collective-permute-start.5 = (f32[2,16,128]{2,1,0:T(8,128)S(1)}, f32[2,16,128]{2,1,0:T(8,128)S(1)}, u32[]{:S(2)}, u32[]{:S(2)}) collective-permute-start(f32[2,16,128]{2,1,0:T(8,128)S(1)} %pad_maximum_fusion.7), channel_id=1, source_target_pairs={{1,0},{2,1},{3,2},{4,3},{5,4},{6,5},{7,6},{9,8},{10,9},{11,10},{12... | collective-permute-start | bytes 49160 | tf_op jit(solution)/shard_map/ppermute | solution.py:17
  41.0 4.0 %collective-permute-start.7 = (f32[2,16,128]{2,1,0:T(8,128)S(1)}, f32[2,16,128]{2,1,0:T(8,128)S(1)}, u32[]{:S(2)}, u32[]{:S(2)}) collective-permute-start(f32[2,16,128]{2,1,0:T(8,128)S(1)} %pad_maximum_fusion.9), channel_id=1, source_target_pairs={{0,8},{8,16},{16,24},{24,32},{32,40},{40,48},{48,56},{1,9},{9,17},... | collective-permute-start | bytes 49160 | tf_op jit(solution)/shard_map/ppermute | solution.py:17
  43.1 5.7 %collective-permute-start.6 = (f32[2,16,128]{2,1,0:T(8,128)S(1)}, f32[2,16,128]{2,1,0:T(8,128)S(1)}, u32[]{:S(2)}, u32[]{:S(2)}) collective-permute-start(f32[2,16,128]{2,1,0:T(8,128)S(1)} %pad_maximum_fusion.8), channel_id=1, source_target_pairs={{0,1},{1,2},{2,3},{3,4},{4,5},{5,6},{6,7},{8,9},{9,10},{10,11},{11... | collective-permute-start | bytes 49160 | tf_op jit(solution)/shard_map/ppermute | solution.py:17
  49.0 1.1 copy-start.3
Sparse Core Ops, SparseCore 0:
  51.3 115.1 all-reduce.9
where the time goes:
time: 311 us; the launch traced here: 310 us
  blocking collectives  134 us (43%)
  waiting for transfers between devices  126 us (41%)
  starting transfers between devices  21.1 us (7%)
  between operations  16.2 us (5%)
  other arithmetic  6.79 us (2%)
  local copies, waits for them, and re-layouts  5.7 us (2%)
    psum x1, blocking collectives, body(): squares = lax.psum(jnp.sum(grad * grad, axis=(1, 2, 3)), ('gx', 'gy'))  134 us
    psum x1, waiting for transfers between devices, body(): grad = lax.psum(term, 'grp')  115 us
    ppermute x8, starting transfers between devices, shifted(): lax.ppermute(value, axis, [(source, source + steps) for source in range(l...  21.1 us
    ppermute x8, waiting for transfers between devices, shifted(): lax.ppermute(value, axis, [(source, source + steps) for source in range(l...  11 us
  transfers between devices with their start and end apart: 9, of which 4 were waited for; matrix products, arithmetic and copies ran while one was open for 2% of the time, Pallas kernels for 0%

commit v1 on v0

v1 whole, which is shorter than its diff:
```python
import functools

import jax
import jax.numpy as jnp
from jax import lax
from jax.experimental import pallas as pl
from jax.experimental.pallas import tpu as pltpu
from jax.sharding import PartitionSpec as P

BS = 8
MESH = pl.DeviceIdType.MESH
F32 = jnp.float32

courant = 0.5
absorb = 0.8

PLANES = 21
ROWS = 24
EX, EY, EZ, HX, HY, HZ, CO, DR = range(8)


def loop(low, count, unroll, step):
    assert count % unroll == 0

    def body(i, carry):
        for u in range(unroll):
            step(low + i * unroll + u)
        return carry

    lax.fori_loop(0, count // unroll, body, 0)


def kernel(
    e_hbm,
    h_hbm,
    fwd_hbm,
    adj_hbm,
    perm_hbm,
    amp_ref,
    plane_ref,
    freq_ref,
    pml_ref,
    blocks_ref,
    grad_hbm,
    scale_ref,
    field,
    damp,
    fwd,
    adj,
    trig,
    weights,
    term,
    landed,
    summed,
    row1,
    rows1,
    row2,
    rows2,
    load_sem,
    halo_send,
    halo_recv,
    red_send,
    red_recv,
    gat_send,
    gat_recv,
    s1_send,
    s1_recv,
    s2_send,
    s2_recv,
    out_sem,
):
    grp = lax.axis_index("grp")
    gx = lax.axis_index("gx")
    gy = lax.axis_index("gy")
    z_hi = grp // 4
    n_x = 8
    n_y = 8

    own = (pl.ds(2, 16), pl.ds(2, 16))
    loads = [
        pltpu.make_async_copy(e_hbm.at[0], field.at[(pl.ds(EX, 3), *own)], load_sem.at[0]),
        pltpu.make_async_copy(h_hbm.at[0], field.at[(pl.ds(HX, 3), *own)], load_sem.at[1]),
        pltpu.make_async_copy(perm_hbm, field.at[(CO, *own)], load_sem.at[2]),
        pltpu.make_async_copy(fwd_hbm.at[0], fwd, load_sem.at[3]),
        pltpu.make_async_copy(adj_hbm.at[0], adj, load_sem.at[4]),
    ]
    for copy in loads:
        copy.start()

    barrier = pltpu.get_barrier_semaphore()
    for d in range(1, 8):
        for axis, me in (("grp", grp), ("gx", gx), ("gy", gy)):
            pl.semaphore_signal(
                barrier, inc=1, device_id={axis: (me + d) % 8}, device_id_type=MESH
            )

    sides = [(dx, dy) for dx in (-1, 0, 1) for dy in (-1, 0, 1) if (dx, dy) != (0, 0)]

    def inside(dx, dy):
        ok = None
        for d, me, n in ((dx, gx, n_x), (dy, gy, n_y)):
            if d != 0:
                here = (me > 0) if d < 0 else (me < n - 1)
                ok = here if ok is None else jnp.logical_and(ok, here)
        return ok

    for dx, dy in sides:
        if dx != 0 and dy != 0:
            pl.semaphore_signal(
                barrier,
                inc=1,
                device_id={"gx": (gx + dx) % n_x, "gy": (gy + dy) % n_y},
                device_id_type=MESH,
            )

    @pl.when(gx == 0)
    def _():
        field[:, 0:2] = jnp.zeros((8, 2, ROWS, 128), F32)

    @pl.when(gx == n_x - 1)
    def _():
        field[:, 18:20] = jnp.zeros((8, 2, ROWS, 128), F32)

    @pl.when(gy == 0)
    def _():
        field[:, 0:20, 0:2, :] = jnp.zeros((8, 20, 2, 128), F32)

    @pl.when(gy == n_y - 1)
    def _():
        field[:, 0:20, 18:20, :] = jnp.zeros((8, 20, 2, 128), F32)

    total_x = n_x * 16
    total_y = n_y * 16

    def profile(cells, total, width):
        place = cells.astype(F32)
        dist = jnp.minimum(place, total - 1.0 - place)
        wide = jnp.full(cells.shape, width, jnp.int32).astype(F32)
        return jnp.maximum(0.0, (wide - dist) / wide) ** 2

    ys = gy * 16 - 2 + lax.broadcasted_iota(jnp.int32, (ROWS, 128), 0)
    prof_y = profile(ys, total_y, pml_ref[1])
    in_y = (ys >= 0) & (ys < total_y)

    def make_damp(p):
        xs = jnp.full((ROWS, 128), gx * 16 - 2 + p, jnp.int32)
        value = jnp.exp(-absorb * (profile(xs, total_x, pml_ref[0]) + prof_y))
        keep = in_y & (xs >= 0) & (xs < total_x)
        damp[p] = jnp.where(keep, value, 0.0)

    loop(0, 20, 4, make_damp)

    row_id = lax.broadcasted_iota(jnp.int32, (8, 128), 0)
    tval = (row_id % 2 + 1).astype(F32)
    omega = jnp.where(
        row_id < 2, jnp.full((8, 128), freq_ref[0, 0]), jnp.full((8, 128), freq_ref[0, 1])
    )
    trig[0:8] = jnp.cos(omega * tval)
    trig[8:16] = jnp.sin(omega * tval)

    eye = lax.broadcasted_iota(jnp.int32, (16, 16), 0) == lax.broadcasted_iota(
        jnp.int32, (16, 16), 1
    )
    lane16 = lax.broadcasted_iota(jnp.int32, (16, 128), 1)
    on_plane = lane16 == plane_ref[0]

    def make_drive(x):
        line = jnp.broadcast_to(amp_ref[0, pl.ds(x, 1), :], (16, 16))
        column = jnp.sum(jnp.where(eye, line, 0.0), axis=1, keepdims=True)
        field[DR, x + 2, pl.ds(2, 16), :] = jnp.where(
            on_plane, jnp.broadcast_to(column, (16, 128)), 0.0
        )

    loop(0, 16, 4, make_drive)

    loads[2].wait()

    def make_coef(p):
        field[CO, p, pl.ds(2, 16), :] = courant / field[CO, p, pl.ds(2, 16), :]

    loop(2, 16, 4, make_coef)

    loads[0].wait()
    loads[1].wait()

    pl.semaphore_wait(barrier, 25)

    def span(d, sending):
        if d == 0:
            return pl.ds(2, 16)
        if sending:
            return pl.ds(2, 2) if d < 0 else pl.ds(16, 2)
        return pl.ds(18, 2) if d < 0 else pl.ds(0, 2)

    def halo(i, dx, dy):
        return pltpu.make_async_remote_copy(
            src_ref=field.at[:, span(dx, True), span(dy, True), :],
            dst_ref=field.at[:, span(dx, False), span(dy, False), :],
            send_sem=halo_send.at[i],
            recv_sem=halo_recv.at[i],
            device_id={"gx": gx + dx, "gy": gy + dy},
            device_id_type=MESH,
        )

    for i, (dx, dy) in enumerate(sides):

        @pl.when(inside(dx, dy))
        def _(i=i, dx=dx, dy=dy):
            halo(i, dx, dy).start()

    loads[3].wait()
    loads[4].wait()

    blocks = blocks_ref[...]
    masks = []
    for bx in range(2):
        for by in range(2):
            cell = (gx * 2 + bx) * (total_y // BS) + gy * 2 + by
            hit = jnp.where(blocks == cell, 1.0, 0.0)
            masks.append(jnp.max(hit, axis=1, keepdims=True))
    upper = lax.broadcasted_iota(jnp.int32, (16, 128), 0) < 8

    def make_weights(bx):
        mask = jnp.where(
            upper,
            jnp.broadcast_to(masks[2 * bx], (16, 128)),
            jnp.broadcast_to(masks[2 * bx + 1], (16, 128)),
        )

        def step(x):
            for k in range(2):
                c1 = trig[pl.ds(2 * k, 1), :]
                c2 = trig[pl.ds(2 * k + 1, 1), :]
                s1 = trig[pl.ds(8 + 2 * k, 1), :]
                s2 = trig[pl.ds(8 + 2 * k + 1, 1), :]
                first = None
                for c in range(3):
                    fr = fwd[k, 0, c, x].astype(F32) * mask
                    fi = fwd[k, 1, c, x].astype(F32) * mask
                    ar = adj[k, 0, c, x].astype(F32)
                    ai = adj[k, 1, c, x].astype(F32)
                    part = fr * ar + fi * ai
                    first = part if first is None else first + part
                    weights[x, k * 7 + 1 + c, pl.ds(2, 16), :] = fr * c1 - fi * s1
                    weights[x, k * 7 + 4 + c, pl.ds(2, 16), :] = fr * c2 - fi * s2
                weights[x, k * 7, pl.ds(2, 16), :] = first

        loop(bx * 8, 8, 1, step)

    make_weights(0)
    make_weights(1)

    for i, (dx, dy) in enumerate(sides):

        @pl.when(inside(dx, dy))
        def _(i=i, dx=dx, dy=dy):
            halo(i, dx, dy).wait_send()

    for i, (dx, dy) in enumerate(sides):

        @pl.when(inside(-dx, -dy))
        def _(i=i, dx=dx, dy=dy):
            halo(i, dx, dy).wait_recv()

    lane = lax.broadcasted_iota(jnp.int32, (ROWS, 128), 1)
    not_last = lane < 127
    not_first = lane > 0

    def ahead_z(v):
        return jnp.where(not_last, pltpu.roll(v, 127, 1), 0.0) - v

    def behind_z(v):
        return v - jnp.where(not_first, pltpu.roll(v, 1, 1), 0.0)

    def ahead_y(v):
        return pltpu.roll(v, ROWS - 1, 0) - v

    def behind_y(v):
        return v - pltpu.roll(v, 1, 0)

    def magnetic(p):
        ex, ey, ez = field[EX, p], field[EY, p], field[EZ, p]
        ey_dx = field[EY, p + 1] - ey
        ez_dx = field[EZ, p + 1] - ez
        d = damp[p]
        field[HX, p] = d * (field[HX, p] - courant * (ahead_y(ez) - ahead_z(ey)))
        field[HY, p] = d * (field[HY, p] - courant * (ahead_z(ex) - ez_dx))
        field[HZ, p] = d * (field[HZ, p] - courant * (ey_dx - ahead_y(ex)))

    def electric(p, sine):
        hx, hy, hz = field[HX, p], field[HY, p], field[HZ, p]
        hy_dx = hy - field[HY, p - 1]
        hz_dx = hz - field[HZ, p - 1]
        d = damp[p]
        co = field[CO, p]
        ex = d * (field[EX, p] + co * (behind_y(hz) - behind_z(hy)))
        ey = d * (field[EY, p] + co * (behind_z(hx) - hz_dx))
        ez = d * (field[EZ, p] + co * (hy_dx - behind_y(hx)) + field[DR, p] * sine)
        return ex, ey, ez

    def electric1(p):
        ex, ey, ez = electric(p, trig[pl.ds(8, 1), :])
        field[EX, p] = ex
        field[EY, p] = ey
        field[EZ, p] = ez

    def electric2(p):
        new = electric(p, trig[pl.ds(9, 1), :])
        old = (field[EX, p], field[EY, p], field[EZ, p])
        x = p - 2
        for k in range(2):
            value = weights[x, k * 7]
            for c in range(3):
                value = value + weights[x, k * 7 + 1 + c] * old[c]
                value = value + weights[x, k * 7 + 4 + c] * new[c]
            term[k, x] = value

    loop(0, 19, 1, magnetic)
    loop(1, 18, 3, electric1)
    loop(1, 17, 1, magnetic)
    loop(2, 16, 2, electric2)

    def piece(j):
        return term.at[j // 4, pl.ds((j % 4) * 4, 4), pl.ds(2, 16), :]

    def reduce_copy(to):
        return pltpu.make_async_remote_copy(
            src_ref=piece(to),
            dst_ref=landed.at[grp],
            send_sem=red_send,
            recv_sem=red_recv,
            device_id={"grp": to},
            device_id_type=MESH,
        )

    for d in (4, 6, 5, 7, 2, 1, 3):
        reduce_copy((grp + d) % 8).start()
    landed[grp] = term[grp // 4, pl.ds((grp % 4) * 4, 4), pl.ds(2, 16), :]
    seven = landed.at[pl.ds(0, 7)]
    pltpu.make_async_copy(seven, seven, red_recv).wait()

    total = landed[0]
    for j in range(1, 8):
        total = total + landed[j]
    summed[grp] = total
    square = jnp.sum(total * total, axis=0)
    line = jnp.sum(square, axis=0, keepdims=True)

    me1 = (grp % 4) * 8 + gy
    me2 = z_hi * 8 + gx
    row1[...] = line
    rows1[pl.ds(me1, 1), :] = line
    for d in range(1, 32):
        to = (me1 + d) % 32
        pltpu.make_async_remote_copy(
            src_ref=row1,
            dst_ref=rows1.at[pl.ds(me1, 1)],
            send_sem=s1_send,
            recv_sem=s1_recv,
            device_id={"grp": z_hi * 4 + to // 8, "gy": to % 8},
            device_id_type=MESH,
        ).start()

    def gather_copy(to):
        return pltpu.make_async_remote_copy(
            src_ref=summed.at[grp],
            dst_ref=summed.at[grp],
            send_sem=gat_send,
            recv_sem=gat_recv,
            device_id={"grp": to},
            device_id_type=MESH,
        )

    for d in (4, 6, 5, 7, 2, 1, 3):
        gather_copy((grp + d) % 8).start()

    some = rows1.at[pl.ds(0, 31)]
    pltpu.make_async_copy(some, some, s1_recv).wait()
    line = jnp.sum(rows1[...], axis=0, keepdims=True)
    row2[...] = line
    rows2[pl.ds(me2, 1), :] = line
    for d in range(1, 16):
        to = (me2 + d) % 16
        pltpu.make_async_remote_copy(
            src_ref=row2,
            dst_ref=rows2.at[pl.ds(me2, 1)],
            send_sem=s2_send,
            recv_sem=s2_recv,
            device_id={"grp": (to // 8) * 4 + grp % 4, "gx": to % 8},
            device_id_type=MESH,
        ).start()

    seven = summed.at[pl.ds(0, 7)]
    pltpu.make_async_copy(seven, seven, gat_recv).wait()
    out = pltpu.make_async_copy(summed, grad_hbm, out_sem)
    out.start()

    few = rows2.at[pl.ds(0, 15)]
    pltpu.make_async_copy(few, few, s2_recv).wait()
    count = float(128 * BS * BS * 128)
    for k in range(2):
        squares = jnp.sum(rows2[8 * k : 8 * k + 8], axis=0, keepdims=True)
        squares = jnp.sum(squares, axis=1, keepdims=True)
        value = lax.rsqrt(squares / count + 1e-05)
        scale_ref[k] = jnp.broadcast_to(value, (8, 128))

    out.wait()
    sent = landed.at[pl.ds(0, 7)]
    pltpu.make_async_copy(sent, sent, red_send).wait()
    pltpu.make_async_copy(seven, seven, gat_send).wait()
    pltpu.make_async_copy(some, some, s1_send).wait()
    pltpu.make_async_copy(few, few, s2_send).wait()


def body(
    efield,
    hfield,
    fwd_dft,
    adj_dft,
    permittivity,
    source_amp,
    source_plane,
    freqs,
    pml_width,
    design_blocks,
):
    hbm = pl.BlockSpec(memory_space=pl.ANY)
    vmem = pl.BlockSpec(memory_space=pltpu.VMEM)
    smem = pl.BlockSpec(memory_space=pltpu.SMEM)
    dma = pltpu.SemaphoreType.DMA
    grad, scale = pl.pallas_call(
        kernel,
        out_shape=(
            jax.ShapeDtypeStruct((8, 4, 16, 128), F32),
            jax.ShapeDtypeStruct((2, 8, 128), F32),
        ),
        in_specs=[hbm, hbm, hbm, hbm, hbm, vmem, smem, smem, smem, vmem],
        out_specs=(hbm, vmem),
        scratch_shapes=[
            pltpu.VMEM((8, PLANES, ROWS, 128), F32),
            pltpu.VMEM((20, ROWS, 128), F32),
            pltpu.VMEM((2, 2, 3, 16, 16, 128), jnp.bfloat16),
            pltpu.VMEM((2, 2, 3, 16, 16, 128), jnp.bfloat16),
            pltpu.VMEM((16, 128), F32),
            pltpu.VMEM((16, 14, ROWS, 128), F32),
            pltpu.VMEM((2, 16, ROWS, 128), F32),
            pltpu.VMEM((8, 4, 16, 128), F32),
            pltpu.VMEM((8, 4, 16, 128), F32),
            pltpu.VMEM((1, 128), F32),
            pltpu.VMEM((32, 128), F32),
            pltpu.VMEM((1, 128), F32),
            pltpu.VMEM((16, 128), F32),
            dma((5,)),
            dma((8,)),
            dma((8,)),
            dma,
            dma,
            dma,
            dma,
            dma,
            dma,
            dma,
            dma,
            dma,
        ],
        compiler_params=pltpu.CompilerParams(
            collective_id=0, has_side_effects=True, vmem_limit_bytes=40 * 1024 * 1024
        ),
        name="adjoint",
    )(
        efield,
        hfield,
        fwd_dft,
        adj_dft,
        permittivity,
        source_amp,
        source_plane,
        freqs,
        pml_width,
        design_blocks[None, :],
    )
    return grad.reshape(2, 16, 16, 128) * scale[:, :1, None, :]


def solution(mesh):
    in_specs = (
        P("grp", None, "gx", "gy", None),
        P("grp", None, "gx", "gy", None),
        P("grp", None, None, None, "gx", "gy", None),
        P("grp", None, None, None, "gx", "gy", None),
        P("gx", "gy", None),
        P("grp", "gx", "gy"),
        P("grp"),
        P("grp", None),
        P(),
        P(),
    )
    out_specs = P(None, "gx", "gy", None)
    return jax.shard_map(body, mesh=mesh, in_specs=in_specs, out_specs=out_specs, check_vma=False)
```

time: 311 us -> 54.9 us (0.18)
  the two profiles are of different devices: /device:TPU:8 before, /device:TPU:1 now
where the time goes in v1:
time: 54.9 us; the launch traced here: 54.6 us
  Pallas kernels  46.6 us (85%)
  local copies, waits for them, and re-layouts  6.52 us (12%)
  other arithmetic  0.72 us (1%)
  between operations  0.7 us (1%)
    pallas_call x1, Pallas kernels, body(): pl.pallas_call(kernel, out_shape=(jax.ShapeDtypeStruct((8, 4, 16, 128), F...  46.6 us
    unnamed x18, local copies, waits for them, and re-layouts  6.52 us

profile of v1, /device:TPU:1, one launch (start us, length us, event | category | flops | bytes accessed | tf_op | source)
XLA Modules:
  0.0 54.6 jit_solution(253051995332219861)
XLA Ops:
  0.7 0.0 copy-start.6
  0.7 0.0 copy-start.7
  0.7 0.0 copy-start.8
  0.7 0.6 %copy-done.6 = f32[1,2]{1,0:T(1,128)S(1)} copy-done((f32[1,2]{1,0:T(1,128)S(1)}, f32[1,2]{1,0:T(1,128)}, u32[]{:S(2)}) %copy-start.6) | copy-done | bytes 32
  1.3 0.0 copy-done.7
  1.3 0.0 copy-done.8
  1.3 0.0 copy-start
  1.3 1.1 %copy-done = bf16[1,2,2,3,16,16,128]{6,5,4,3,2,1,0:T(8,128)(2,1)S(1)} copy-done((bf16[1,2,2,3,16,16,128]{6,5,4,3,2,1,0:T(8,128)(2,1)S(1)}, bf16[1,2,2,3,16,16,128]{6,5,4,3,2,1,0:T(8,128)(2,1)}, u32[]{:S(2)}) %copy-start) | copy-done | bytes 786456
  2.5 0.0 copy-start.1
  2.5 1.1 %copy-done.1 = bf16[1,2,2,3,16,16,128]{6,5,4,3,2,1,0:T(8,128)(2,1)S(1)} copy-done((bf16[1,2,2,3,16,16,128]{6,5,4,3,2,1,0:T(8,128)(2,1)S(1)}, bf16[1,2,2,3,16,16,128]{6,5,4,3,2,1,0:T(8,128)(2,1)}, u32[]{:S(2)}) %copy-start.1) | copy-done | bytes 786456
  3.6 0.0 copy-start.2
  3.6 1.0 %copy-done.2 = f32[1,3,16,16,128]{4,3,2,1,0:T(8,128)S(1)} copy-done((f32[1,3,16,16,128]{4,3,2,1,0:T(8,128)S(1)}, f32[1,3,16,16,128]{4,3,2,1,0:T(8,128)}, u32[]{:S(2)}) %copy-start.2) | copy-done | bytes 393240
  4.6 0.0 copy-start.3
  4.6 1.0 %copy-done.3 = f32[1,3,16,16,128]{4,3,2,1,0:T(8,128)S(1)} copy-done((f32[1,3,16,16,128]{4,3,2,1,0:T(8,128)S(1)}, f32[1,3,16,16,128]{4,3,2,1,0:T(8,128)}, u32[]{:S(2)}) %copy-start.3) | copy-done | bytes 393240
  5.6 0.0 copy-start.4
  5.6 0.9 %copy-done.4 = f32[16,16,128]{2,1,0:T(8,128)S(1)} copy-done((f32[16,16,128]{2,1,0:T(8,128)S(1)}, f32[16,16,128]{2,1,0:T(8,128)}, u32[]{:S(2)}) %copy-start.4) | copy-done | bytes 131096
  6.5 0.0 copy-start.5
  6.5 0.7 %copy-done.5 = f32[1,16,16]{2,1,0:T(8,128)S(1)} copy-done((f32[1,16,16]{2,1,0:T(8,128)S(1)}, f32[1,16,16]{2,1,0:T(8,128)}, u32[]{:S(2)}) %copy-start.5) | copy-done | bytes 1048
  7.2 46.6 %adjoint.1 = (f32[8,4,16,128]{3,2,1,0:T(8,128)S(1)}, f32[2,8,128]{2,1,0:T(8,128)S(1)}) custom-call(f32[1,3,16,16,128]{4,3,2,1,0:T(8,128)S(1)} %copy-done.2, f32[1,3,16,16,128]{4,3,2,1,0:T(8,128)S(1)} %copy-done.3, bf16[1,2,2,3,16,16,128]{6,5,4,3,2,1,0:T(8,128)(2,1)S(1)} %copy-done, bf16[1,2,2,3,16,16,128]{6,5,4,3,2,1,0:T(8,128)(2,1)S(1)} %copy-done.1, ...), custom_call_target="tpu_custom_call" | custom-call | tf_op jit(solution)/shard_map/adjoint/pallas_call | solution.py:431
  53.8 0.7 %bitcast_multiply_fusion = f32[2,16,16,128]{3,2,1,0:T(8,128)} fusion(f32[2,128]{1,0:T(2,128)S(1)} %bitcast.7, f32[2,16,16,128]{3,2,1,0:T(8,128)S(1)} %bitcast.5), kind=kLoop, calls=%fused_computation | loop fusion | flops 65536 | bytes 525312 | tf_op jit(solution)/shard_map/mul | solution.py:482
  (1 shorter events, 0.0 us)
Async XLA Ops:
  0.7 0.7 %copy-start.6 = (f32[1,2]{1,0:T(1,128)S(1)}, f32[1,2]{1,0:T(1,128)}, u32[]{:S(2)}) copy-start(f32[1,2]{1,0:T(1,128)} %freq_ref.1) | copy-start | bytes 28
  0.7 0.7 %copy-start.7 = (s32[2]{0:T(128)S(1)}, s32[2]{0:T(128)}, u32[]{:S(2)}) copy-start(s32[2]{0:T(128)} %pml_ref.1) | copy-start | bytes 28
  0.7 0.7 %copy-start.8 = (s32[128]{0:T(128)S(1)}, s32[128]{0:T(128)}, u32[]{:S(2)}) copy-start(s32[128]{0:T(128)} %param.19) | copy-start | bytes 1540
  1.3 1.1 %copy-start = (bf16[1,2,2,3,16,16,128]{6,5,4,3,2,1,0:T(8,128)(2,1)S(1)}, bf16[1,2,2,3,16,16,128]{6,5,4,3,2,1,0:T(8,128)(2,1)}, u32[]{:S(2)}) copy-start(bf16[1,2,2,3,16,16,128]{6,5,4,3,2,1,0:T(8,128)(2,1)} %fwd_hbm.1) | copy-start | bytes 2359300
  2.5 1.1 %copy-start.1 = (bf16[1,2,2,3,16,16,128]{6,5,4,3,2,1,0:T(8,128)(2,1)S(1)}, bf16[1,2,2,3,16,16,128]{6,5,4,3,2,1,0:T(8,128)(2,1)}, u32[]{:S(2)}) copy-start(bf16[1,2,2,3,16,16,128]{6,5,4,3,2,1,0:T(8,128)(2,1)} %adj_hbm.1) | copy-start | bytes 2359300
  3.6 1.0 %copy-start.2 = (f32[1,3,16,16,128]{4,3,2,1,0:T(8,128)S(1)}, f32[1,3,16,16,128]{4,3,2,1,0:T(8,128)}, u32[]{:S(2)}) copy-start(f32[1,3,16,16,128]{4,3,2,1,0:T(8,128)} %e_hbm.1) | copy-start | bytes 1179652
  4.6 1.0 %copy-start.3 = (f32[1,3,16,16,128]{4,3,2,1,0:T(8,128)S(1)}, f32[1,3,16,16,128]{4,3,2,1,0:T(8,128)}, u32[]{:S(2)}) copy-start(f32[1,3,16,16,128]{4,3,2,1,0:T(8,128)} %h_hbm.1) | copy-start | bytes 1179652
  5.6 0.9 %copy-start.4 = (f32[16,16,128]{2,1,0:T(8,128)S(1)}, f32[16,16,128]{2,1,0:T(8,128)}, u32[]{:S(2)}) copy-start(f32[16,16,128]{2,1,0:T(8,128)} %perm_hbm.1) | copy-start | bytes 393220
  6.5 0.7 %copy-start.5 = (f32[1,16,16]{2,1,0:T(8,128)S(1)}, f32[1,16,16]{2,1,0:T(8,128)}, u32[]{:S(2)}) copy-start(f32[1,16,16]{2,1,0:T(8,128)} %amp_ref.1) | copy-start | bytes 3076

commit v2 on v1

--- a/solution.py
+++ b/solution.py
@@ -36,11 +36,11 @@
     fwd_hbm,
     adj_hbm,
     perm_hbm,
-    amp_ref,
+    amp_hbm,
     plane_ref,
-    freq_ref,
-    pml_ref,
-    blocks_ref,
+    freq_hbm,
+    pml_hbm,
+    blocks_hbm,
     grad_hbm,
     scale_ref,
     field,
@@ -56,6 +56,10 @@
     rows1,
     row2,
     rows2,
+    amp_ref,
+    freq_ref,
+    pml_ref,
+    blocks_ref,
     load_sem,
     halo_send,
     halo_recv,
@@ -76,6 +80,20 @@
     n_x = 8
     n_y = 8
 
+    sides = [(dx, dy) for dx in (-1, 0, 1) for dy in (-1, 0, 1) if (dx, dy) != (0, 0)]
+    barrier = pltpu.get_barrier_semaphore()
+
+    def greet(device):
+        pl.semaphore_signal(barrier, inc=1, device_id=device, device_id_type=MESH)
+
+    for dx, dy in sides:
+        device = {}
+        if dx != 0:
+            device["gx"] = (gx + dx) % n_x
+        if dy != 0:
+            device["gy"] = (gy + dy) % n_y
+        greet(device)
+
     own = (pl.ds(2, 16), pl.ds(2, 16))
     loads = [
         pltpu.make_async_copy(e_hbm.at[0], field.at[(pl.ds(EX, 3), *own)], load_sem.at[0]),
@@ -83,18 +101,21 @@
         pltpu.make_async_copy(perm_hbm, field.at[(CO, *own)], load_sem.at[2]),
         pltpu.make_async_copy(fwd_hbm.at[0], fwd, load_sem.at[3]),
         pltpu.make_async_copy(adj_hbm.at[0], adj, load_sem.at[4]),
+        pltpu.make_async_copy(pml_hbm, pml_ref, load_sem.at[5]),
+        pltpu.make_async_copy(freq_hbm, freq_ref, load_sem.at[6]),
+        pltpu.make_async_copy(amp_hbm, amp_ref, load_sem.at[7]),
+        pltpu.make_async_copy(blocks_hbm, blocks_ref, load_sem.at[8]),
     ]
-    for copy in loads:
-        copy.start()
-
-    barrier = pltpu.get_barrier_semaphore()
-    for d in range(1, 8):
-        for axis, me in (("grp", grp), ("gx", gx), ("gy", gy)):
-            pl.semaphore_signal(
-                barrier, inc=1, device_id={axis: (me + d) % 8}, device_id_type=MESH
-            )
-
-    sides = [(dx, dy) for dx in (-1, 0, 1) for dy in (-1, 0, 1) if (dx, dy) != (0, 0)]
+    for i in (5, 2, 7, 0, 1, 6, 3, 4, 8):
+        loads[i].start()
+
+    for d in range(4, 8):
+        greet({"grp": (grp + d) % 8})
+    for d in range(1, 4):
+        greet({"grp": (grp + d) % 8})
+    for d in range(2, 7):
+        greet({"gx": (gx + d) % 8})
+        greet({"gy": (gy + d) % 8})
 
     def inside(dx, dy):
         ok = None
@@ -104,15 +125,6 @@
                 ok = here if ok is None else jnp.logical_and(ok, here)
         return ok
 
-    for dx, dy in sides:
-        if dx != 0 and dy != 0:
-            pl.semaphore_signal(
-                barrier,
-                inc=1,
-                device_id={"gx": (gx + dx) % n_x, "gy": (gy + dy) % n_y},
-                device_id_type=MESH,
-            )
-
     @pl.when(gx == 0)
     def _():
         field[:, 0:2] = jnp.zeros((8, 2, ROWS, 128), F32)
@@ -138,6 +150,7 @@
         wide = jnp.full(cells.shape, width, jnp.int32).astype(F32)
         return jnp.maximum(0.0, (wide - dist) / wide) ** 2
 
+    loads[5].wait()
     ys = gy * 16 - 2 + lax.broadcasted_iota(jnp.int32, (ROWS, 128), 0)
     prof_y = profile(ys, total_y, pml_ref[1])
     in_y = (ys >= 0) & (ys < total_y)
@@ -150,17 +163,10 @@
 
     loop(0, 20, 4, make_damp)
 
-    row_id = lax.broadcasted_iota(jnp.int32, (8, 128), 0)
-    tval = (row_id % 2 + 1).astype(F32)
-    omega = jnp.where(
-        row_id < 2, jnp.full((8, 128), freq_ref[0, 0]), jnp.full((8, 128), freq_ref[0, 1])
-    )
-    trig[0:8] = jnp.cos(omega * tval)
-    trig[8:16] = jnp.sin(omega * tval)
-
     eye = lax.broadcasted_iota(jnp.int32, (16, 16), 0) == lax.broadcasted_iota(
         jnp.int32, (16, 16), 1
     )
+    loads[7].wait()
     lane16 = lax.broadcasted_iota(jnp.int32, (16, 128), 1)
     on_plane = lane16 == plane_ref[0]
 
@@ -208,6 +214,16 @@
         def _(i=i, dx=dx, dy=dy):
             halo(i, dx, dy).start()
 
+    loads[6].wait()
+    row_id = lax.broadcasted_iota(jnp.int32, (8, 128), 0)
+    tval = (row_id % 2 + 1).astype(F32)
+    omega = jnp.where(
+        row_id < 2, jnp.full((8, 128), freq_ref[0, 0]), jnp.full((8, 128), freq_ref[0, 1])
+    )
+    trig[0:8] = jnp.cos(omega * tval)
+    trig[8:16] = jnp.sin(omega * tval)
+
+    loads[8].wait()
     loads[3].wait()
     loads[4].wait()
 
@@ -278,54 +294,32 @@
     def behind_y(v):
         return v - pltpu.roll(v, 1, 0)
 
-    def magnetic(p):
-        ex, ey, ez = field[EX, p], field[EY, p], field[EZ, p]
-        ey_dx = field[EY, p + 1] - ey
-        ez_dx = field[EZ, p + 1] - ez
+    def magnetic(p, e, ahead, h):
         d = damp[p]
-        field[HX, p] = d * (field[HX, p] - courant * (ahead_y(ez) - ahead_z(ey)))
-        field[HY, p] = d * (field[HY, p] - courant * (ahead_z(ex) - ez_dx))
-        field[HZ, p] = d * (field[HZ, p] - courant * (ey_dx - ahead_y(ex)))
-
-    def electric(p, sine):
-        hx, hy, hz = field[HX, p], field[HY, p], field[HZ, p]
-        hy_dx = hy - field[HY, p - 1]
-        hz_dx = hz - field[HZ, p - 1]
+        ex, ey, ez = e
+        hx = d * (h[0] - courant * (ahead_y(ez) - ahead_z(ey)))
+        hy = d * (h[1] - courant * (ahead_z(ex) - (ahead[2] - ez)))
+        hz = d * (h[2] - courant * ((ahead[1] - ey) - ahead_y(ex)))
+        return hx, hy, hz
+
+    def electric(p, h, behind, e, sine):
         d = damp[p]
         co = field[CO, p]
-        ex = d * (field[EX, p] + co * (behind_y(hz) - behind_z(hy)))
-        ey = d * (field[EY, p] + co * (behind_z(hx) - hz_dx))
-        ez = d * (field[EZ, p] + co * (hy_dx - behind_y(hx)) + field[DR, p] * sine)
+        hx, hy, hz = h
+        ex = d * (e[0] + co * (behind_y(hz) - behind_z(hy)))
+        ey = d * (e[1] + co * (behind_z(hx) - (hz - behind[2])))
+        ez = d * (e[2] + co * ((hy - behind[1]) - behind_y(hx)) + field[DR, p] * sine)
         return ex, ey, ez
 
-    def electric1(p):
-        ex, ey, ez = electric(p, trig[pl.ds(8, 1), :])
-        field[EX, p] = ex
-        field[EY, p] = ey
-        field[EZ, p] = ez
-
-    def electric2(p):
-        new = electric(p, trig[pl.ds(9, 1), :])
-        old = (field[EX, p], field[EY, p], field[EZ, p])
-        x = p - 2
-        for k in range(2):
-            value = weights[x, k * 7]
-            for c in range(3):
-                value = value + weights[x, k * 7 + 1 + c] * old[c]
-                value = value + weights[x, k * 7 + 4 + c] * new[c]
-            term[k, x] = value
-
-    loop(0, 19, 1, magnetic)
-    loop(1, 18, 3, electric1)
-    loop(1, 17, 1, magnetic)
-    loop(2, 16, 2, electric2)
-
-    def piece(j):
-        return term.at[j // 4, pl.ds((j % 4) * 4, 4), pl.ds(2, 16), :]
+    sine1 = trig[pl.ds(8, 1), :]
+    sine2 = trig[pl.ds(9, 1), :]
+
+    def read(first, p):
+        return tuple(field[first + c, p] for c in range(3))
 
     def reduce_copy(to):
         return pltpu.make_async_remote_copy(
-            src_ref=piece(to),
+            src_ref=term.at[to // 4, pl.ds((to % 4) * 4, 4), pl.ds(2, 16), :],
             dst_ref=landed.at[grp],
             send_sem=red_send,
             recv_sem=red_recv,
@@ -333,9 +327,40 @@
             device_id_type=MESH,
         )
 
-    for d in (4, 6, 5, 7, 2, 1, 3):
-        reduce_copy((grp + d) % 8).start()
-    landed[grp] = term[grp // 4, pl.ds((grp % 4) * 4, 4), pl.ds(2, 16), :]
+    def send_quarter(q):
+        for to in (q, q + 4):
+
+            @pl.when(grp != to)
+            def _():
+                reduce_copy(to).start()
+
+            @pl.when(grp == to)
+            def _():
+                landed[to] = term[to // 4, 4 * (to % 4) : 4 * (to % 4) + 4, 2:18, :]
+
+    e0 = read(EX, 0)
+    h1 = e1 = h2 = None
+    for p in range(19):
+        e0_next = read(EX, p + 1)
+        h1_last, e1_last, h2_last = h1, e1, h2
+        h1 = magnetic(p, e0, e0_next, read(HX, p))
+        if p >= 1:
+            e1 = electric(p, h1, h1_last, e0, sine1)
+        if p >= 2:
+            h2 = magnetic(p - 1, e1_last, e1, h1_last)
+        if p >= 3:
+            e2 = electric(p - 1, h2, h2_last, e1_last, sine2)
+            x = p - 3
+            for k in range(2):
+                value = weights[x, k * 7]
+                for c in range(3):
+                    value = value + weights[x, k * 7 + 1 + c] * e1_last[c]
+                    value = value + weights[x, k * 7 + 4 + c] * e2[c]
+                term[k, x] = value
+            if x % 4 == 3:
+                send_quarter(x // 4)
+        e0 = e0_next
+
     seven = landed.at[pl.ds(0, 7)]
     pltpu.make_async_copy(seven, seven, red_recv).wait()
 
@@ -424,9 +449,11 @@
     pml_width,
     design_blocks,
 ):
-    hbm = pl.BlockSpec(memory_space=pl.ANY)
+    hbm = pl.BlockSpec(memory_space=pltpu.HBM)
+    def pin(value):
+        return pltpu.with_memory_space_constraint(value, pltpu.HBM)
+
     vmem = pl.BlockSpec(memory_space=pltpu.VMEM)
-    smem = pl.BlockSpec(memory_space=pltpu.SMEM)
     dma = pltpu.SemaphoreType.DMA
     grad, scale = pl.pallas_call(
         kernel,
@@ -434,8 +461,8 @@
             jax.ShapeDtypeStruct((8, 4, 16, 128), F32),
             jax.ShapeDtypeStruct((2, 8, 128), F32),
         ),
-        in_specs=[hbm, hbm, hbm, hbm, hbm, vmem, smem, smem, smem, vmem],
-        out_specs=(hbm, vmem),
+        in_specs=[hbm] * 6 + [pl.BlockSpec(memory_space=pltpu.SMEM)] + [hbm] * 3,
+        out_specs=(pl.BlockSpec(memory_space=pl.ANY), vmem),
         scratch_shapes=[
             pltpu.VMEM((8, PLANES, ROWS, 128), F32),
             pltpu.VMEM((20, ROWS, 128), F32),
@@ -450,7 +477,11 @@
             pltpu.VMEM((32, 128), F32),
             pltpu.VMEM((1, 128), F32),
             pltpu.VMEM((16, 128), F32),
-            dma((5,)),
+            pltpu.VMEM((1, 16, 16), F32),
+            pltpu.SMEM((1, 2), F32),
+            pltpu.SMEM((2,), jnp.int32),
+            pltpu.VMEM((1, 128), jnp.int32),
+            dma((9,)),
             dma((8,)),
             dma((8,)),
             dma,
@@ -468,16 +499,9 @@
         ),
         name="adjoint",
     )(
-        efield,
-        hfield,
-        fwd_dft,
-        adj_dft,
-        permittivity,
-        source_amp,
+        *map(pin, (efield, hfield, fwd_dft, adj_dft, permittivity, source_amp)),
         source_plane,
-        freqs,
-        pml_width,
-        design_blocks[None, :],
+        *map(pin, (freqs, pml_width, design_blocks[None, :])),
     )
     return grad.reshape(2, 16, 16, 128) * scale[:, :1, None, :]
 

time: 54.9 us -> 46.5 us (0.85)
  local copies, waits for them, and re-layouts: 6.52 us -> 0.01 us
  Pallas kernels: 46.6 us -> 45 us
    unnamed x18 -> x0, local copies, waits for them, and re-layouts: 6.52 us -> none
    pallas_call x1, Pallas kernels: 46.6 us -> 45 us  [body(): pl.pallas_call(kernel, out_shape=(jax.ShapeDtypeStruct((8, 4, 16, 128), F...]
where the time goes in v2:
time: 46.5 us; the launch traced here: 46.4 us
  Pallas kernels  45 us (97%)
  other arithmetic  0.72 us (2%)
  between operations  0.67 us (1%)
    pallas_call x1, Pallas kernels, body(): pl.pallas_call(kernel, out_shape=(jax.ShapeDtypeStruct((8, 4, 16, 128), F...  45 us

profile of v2, /device:TPU:1, one launch (start us, length us, event | category | flops | bytes accessed | tf_op | source)
XLA Modules:
  0.0 46.4 jit_solution(3679628465499230681)
XLA Ops:
  0.7 45.0 %adjoint.1 = (f32[8,4,16,128]{3,2,1,0:T(8,128)S(1)}, f32[2,8,128]{2,1,0:T(8,128)S(1)}) custom-call(f32[1,3,16,16,128]{4,3,2,1,0:T(8,128)} %e_hbm.1, f32[1,3,16,16,128]{4,3,2,1,0:T(8,128)} %h_hbm.1, bf16[1,2,2,3,16,16,128]{6,5,4,3,2,1,0:T(8,128)(2,1)} %fwd_hbm.1, bf16[1,2,2,3,16,16,128]{6,5,4,3,2,1,0:T(8,128)(2,1)} %adj_hbm.1, f32[16,16,128]{2,1,0:T(8,128)} %perm_hbm.1, ...), custom_call_target="tpu_custom_call" | custom-call | tf_op jit(solution)/shard_map/adjoint/pallas_call | solution.py:458
  45.7 0.7 %bitcast_multiply_fusion = f32[2,16,16,128]{3,2,1,0:T(8,128)} fusion(f32[2,128]{1,0:T(2,128)S(1)} %bitcast.6, f32[2,16,16,128]{3,2,1,0:T(8,128)S(1)} %bitcast.5), kind=kLoop, calls=%fused_computation | loop fusion | flops 65536 | bytes 525312 | tf_op jit(solution)/shard_map/mul | solution.py:506
  (1 shorter events, 0.0 us)

commit v3 on v2

--- a/solution.py
+++ b/solution.py
@@ -125,6 +125,77 @@
                 ok = here if ok is None else jnp.logical_and(ok, here)
         return ok
 
+    pl.semaphore_wait(barrier, 25)
+
+    def pick(d, wide):
+        if d == 0:
+            return pl.ds(0, 16), pl.ds(2, 16)
+        if d > 0:
+            return pl.ds(16 - wide, wide), pl.ds(2 - wide, wide)
+        return pl.ds(0, wide), pl.ds(18, wide)
+
+    e_arg, h_arg = e_hbm.at[0], h_hbm.at[0]
+    parts = {
+        (1, 0): [(e_arg, EX, 0, 3, 2, 0), (h_arg, HX, 1, 2, 2, 0), (h_arg, HX, 0, 1, 1, 0)],
+        (-1, 0): [(e_arg, EX, 1, 2, 2, 0), (h_arg, HX, 0, 3, 1, 0), (e_arg, EX, 0, 1, 1, 0)],
+        (0, 1): [(e_arg, EX, 0, 3, 0, 2), (h_arg, HX, 0, 3, 0, 2)],
+        (0, -1): [(e_arg, EX, 0, 3, 0, 2), (h_arg, HX, 0, 3, 0, 1)],
+        (1, 1): [(e_arg, EX, 0, 3, 1, 1), (h_arg, HX, 0, 3, 1, 1)],
+        (1, -1): [(e_arg, EX, 0, 3, 2, 2), (h_arg, HX, 0, 3, 1, 1)],
+        (-1, 1): [(e_arg, EX, 0, 3, 2, 2), (h_arg, HX, 0, 3, 1, 1)],
+        (-1, -1): [(e_arg, EX, 0, 3, 1, 1)],
+    }
+
+    def halo(dx, dy):
+        copies = []
+        for i, (source, base, first, many, wide_x, wide_y) in enumerate(parts[dx, dy]):
+            from_x, to_x = pick(dx, wide_x)
+            from_y, to_y = pick(dy, wide_y)
+            slot = 3 * sides.index((dx, dy)) + i
+            copies.append(
+                pltpu.make_async_remote_copy(
+                    src_ref=source.at[pl.ds(first, many), from_x, from_y, :],
+                    dst_ref=field.at[pl.ds(base + first, many), to_x, to_y, :],
+                    send_sem=halo_send.at[slot],
+                    recv_sem=halo_recv.at[slot],
+                    device_id={"gx": gx + dx, "gy": gy + dy},
+                    device_id_type=MESH,
+                )
+            )
+        return copies
+
+    def aux(dx, dy):
+        from_x, to_x = pick(dx, 1)
+        from_y, to_y = pick(dy, 1)
+        slot = 24 + sides.index((dx, dy))
+        inner_x = pl.ds(from_x.start + 2, from_x.size)
+        inner_y = pl.ds(from_y.start + 2, from_y.size)
+        return pltpu.make_async_remote_copy(
+            src_ref=field.at[pl.ds(CO, 2), inner_x, inner_y, :],
+            dst_ref=field.at[pl.ds(CO, 2), to_x, to_y, :],
+            send_sem=halo_send.at[slot],
+            recv_sem=halo_recv.at[slot],
+            device_id={"gx": gx + dx, "gy": gy + dy},
+            device_id_type=MESH,
+        )
+
+    order = [(0, 1), (0, -1), (1, 0), (-1, 0), (1, -1), (-1, 1), (1, 1), (-1, -1)]
+    aux_order = [side for side in order if side not in ((1, 1), (-1, -1))]
+
+    for dx, dy in order:
+
+        @pl.when(inside(dx, dy))
+        def _(dx=dx, dy=dy):
+            for copy in halo(dx, dy):
+                copy.start()
+
+    def start_aux():
+        for dx, dy in aux_order:
+
+            @pl.when(inside(dx, dy))
+            def _(dx=dx, dy=dy):
+                aux(dx, dy).start()
+
     @pl.when(gx == 0)
     def _():
         field[:, 0:2] = jnp.zeros((8, 2, ROWS, 128), F32)
@@ -140,28 +211,6 @@
     @pl.when(gy == n_y - 1)
     def _():
         field[:, 0:20, 18:20, :] = jnp.zeros((8, 20, 2, 128), F32)
-
-    total_x = n_x * 16
-    total_y = n_y * 16
-
-    def profile(cells, total, width):
-        place = cells.astype(F32)
-        dist = jnp.minimum(place, total - 1.0 - place)
-        wide = jnp.full(cells.shape, width, jnp.int32).astype(F32)
-        return jnp.maximum(0.0, (wide - dist) / wide) ** 2
-
-    loads[5].wait()
-    ys = gy * 16 - 2 + lax.broadcasted_iota(jnp.int32, (ROWS, 128), 0)
-    prof_y = profile(ys, total_y, pml_ref[1])
-    in_y = (ys >= 0) & (ys < total_y)
-
-    def make_damp(p):
-        xs = jnp.full((ROWS, 128), gx * 16 - 2 + p, jnp.int32)
-        value = jnp.exp(-absorb * (profile(xs, total_x, pml_ref[0]) + prof_y))
-        keep = in_y & (xs >= 0) & (xs < total_x)
-        damp[p] = jnp.where(keep, value, 0.0)
-
-    loop(0, 20, 4, make_damp)
 
     eye = lax.broadcasted_iota(jnp.int32, (16, 16), 0) == lax.broadcasted_iota(
         jnp.int32, (16, 16), 1
@@ -186,33 +235,29 @@
 
     loop(2, 16, 4, make_coef)
 
-    loads[0].wait()
-    loads[1].wait()
-
-    pl.semaphore_wait(barrier, 25)
-
-    def span(d, sending):
-        if d == 0:
-            return pl.ds(2, 16)
-        if sending:
-            return pl.ds(2, 2) if d < 0 else pl.ds(16, 2)
-        return pl.ds(18, 2) if d < 0 else pl.ds(0, 2)
-
-    def halo(i, dx, dy):
-        return pltpu.make_async_remote_copy(
-            src_ref=field.at[:, span(dx, True), span(dy, True), :],
-            dst_ref=field.at[:, span(dx, False), span(dy, False), :],
-            send_sem=halo_send.at[i],
-            recv_sem=halo_recv.at[i],
-            device_id={"gx": gx + dx, "gy": gy + dy},
-            device_id_type=MESH,
-        )
-
-    for i, (dx, dy) in enumerate(sides):
-
-        @pl.when(inside(dx, dy))
-        def _(i=i, dx=dx, dy=dy):
-            halo(i, dx, dy).start()
+    start_aux()
+
+    total_x = n_x * 16
+    total_y = n_y * 16
+
+    def profile(cells, total, width):
+        place = cells.astype(F32)
+        dist = jnp.minimum(place, total - 1.0 - place)
+        wide = jnp.full(cells.shape, width, jnp.int32).astype(F32)
+        return jnp.maximum(0.0, (wide - dist) / wide) ** 2
+
+    loads[5].wait()
+    ys = gy * 16 - 2 + lax.broadcasted_iota(jnp.int32, (ROWS, 128), 0)
+    prof_y = profile(ys, total_y, pml_ref[1])
+    in_y = (ys >= 0) & (ys < total_y)
+
+    def make_damp(p):
+        xs = jnp.full((ROWS, 128), gx * 16 - 2 + p, jnp.int32)
+        value = jnp.exp(-absorb * (profile(xs, total_x, pml_ref[0]) + prof_y))
+        keep = in_y & (xs >= 0) & (xs < total_x)
+        damp[p] = jnp.where(keep, value, 0.0)
+
+    loop(0, 20, 4, make_damp)
 
     loads[6].wait()
     row_id = lax.broadcasted_iota(jnp.int32, (8, 128), 0)
@@ -266,17 +311,17 @@
     make_weights(0)
     make_weights(1)
 
-    for i, (dx, dy) in enumerate(sides):
-
-        @pl.when(inside(dx, dy))
-        def _(i=i, dx=dx, dy=dy):
-            halo(i, dx, dy).wait_send()
-
-    for i, (dx, dy) in enumerate(sides):
+    loads[0].wait()
+    loads[1].wait()
+
+    for dx, dy in order:
 
         @pl.when(inside(-dx, -dy))
-        def _(i=i, dx=dx, dy=dy):
-            halo(i, dx, dy).wait_recv()
+        def _(dx=dx, dy=dy):
+            for copy in halo(dx, dy):
+                copy.wait_recv()
+            if (dx, dy) in aux_order:
+                aux(dx, dy).wait_recv()
 
     lane = lax.broadcasted_iota(jnp.int32, (ROWS, 128), 1)
     not_last = lane < 127
@@ -317,26 +362,23 @@
     def read(first, p):
         return tuple(field[first + c, p] for c in range(3))
 
-    def reduce_copy(to):
-        return pltpu.make_async_remote_copy(
-            src_ref=term.at[to // 4, pl.ds((to % 4) * 4, 4), pl.ds(2, 16), :],
-            dst_ref=landed.at[grp],
-            send_sem=red_send,
-            recv_sem=red_recv,
-            device_id={"grp": to},
-            device_id_type=MESH,
-        )
+    lane_x = grp % 4
+    others = [(1, 2), (1, 1), (1, 3), (1, 0), (0, 2), (0, 1), (0, 3)]
+
+    def peer(dz, dx):
+        return (z_hi + dz) % 2, (lane_x + dx) % 4
 
     def send_quarter(q):
-        for to in (q, q + 4):
-
-            @pl.when(grp != to)
-            def _():
-                reduce_copy(to).start()
-
-            @pl.when(grp == to)
-            def _():
-                landed[to] = term[to // 4, 4 * (to % 4) : 4 * (to % 4) + 4, 2:18, :]
+        for dz, dx in others:
+            k, j = peer(dz, dx)
+            pltpu.make_async_remote_copy(
+                src_ref=term.at[k, 4 * q + j, pl.ds(2, 16), :],
+                dst_ref=landed.at[grp, q],
+                send_sem=red_send,
+                recv_sem=red_recv,
+                device_id={"grp": k * 4 + j},
+                device_id_type=MESH,
+            ).start()
 
     e0 = read(EX, 0)
     h1 = e1 = h2 = None
@@ -361,61 +403,66 @@
                 send_quarter(x // 4)
         e0 = e0_next
 
+    for q in range(4):
+        landed[grp, q] = term[z_hi, 4 * q + lane_x, 2:18, :]
     seven = landed.at[pl.ds(0, 7)]
     pltpu.make_async_copy(seven, seven, red_recv).wait()
 
     total = landed[0]
     for j in range(1, 8):
         total = total + landed[j]
-    summed[grp] = total
+    summed[z_hi, :, lane_x] = total
     square = jnp.sum(total * total, axis=0)
     line = jnp.sum(square, axis=0, keepdims=True)
 
-    me1 = (grp % 4) * 8 + gy
+    me1 = lane_x * 8 + gy
     me2 = z_hi * 8 + gx
     row1[...] = line
     rows1[pl.ds(me1, 1), :] = line
-    for d in range(1, 32):
-        to = (me1 + d) % 32
+    steps = [(dx, dy) for dx in range(4) for dy in range(8) if (dx, dy) != (0, 0)]
+    for dx, dy in sorted(steps, key=lambda d: -min(d[0], 4 - d[0]) - min(d[1], 8 - d[1])):
         pltpu.make_async_remote_copy(
             src_ref=row1,
             dst_ref=rows1.at[pl.ds(me1, 1)],
             send_sem=s1_send,
             recv_sem=s1_recv,
-            device_id={"grp": z_hi * 4 + to // 8, "gy": to % 8},
+            device_id={"grp": z_hi * 4 + (lane_x + dx) % 4, "gy": (gy + dy) % 8},
             device_id_type=MESH,
         ).start()
 
-    def gather_copy(to):
-        return pltpu.make_async_remote_copy(
-            src_ref=summed.at[grp],
-            dst_ref=summed.at[grp],
+    mine = summed.at[z_hi, :, lane_x]
+    for dz, dx in others:
+        k, j = peer(dz, dx)
+        pltpu.make_async_remote_copy(
+            src_ref=mine,
+            dst_ref=mine,
             send_sem=gat_send,
             recv_sem=gat_recv,
-            device_id={"grp": to},
+            device_id={"grp": k * 4 + j},
             device_id_type=MESH,
-        )
-
-    for d in (4, 6, 5, 7, 2, 1, 3):
-        gather_copy((grp + d) % 8).start()
+        ).start()
 
     some = rows1.at[pl.ds(0, 31)]
     pltpu.make_async_copy(some, some, s1_recv).wait()
     line = jnp.sum(rows1[...], axis=0, keepdims=True)
     row2[...] = line
     rows2[pl.ds(me2, 1), :] = line
-    for d in range(1, 16):
-        to = (me2 + d) % 16
+    place = me2 // 2
+    steps = [(dz, dc) for dz in range(8) for dc in range(2) if (dz, dc) != (0, 0)]
+    for dz, dc in sorted(steps, key=lambda d: -min(d[0], 8 - d[0])):
+        to_z = (place + dz) % 8
         pltpu.make_async_remote_copy(
             src_ref=row2,
             dst_ref=rows2.at[pl.ds(me2, 1)],
             send_sem=s2_send,
             recv_sem=s2_recv,
-            device_id={"grp": (to // 8) * 4 + grp % 4, "gx": to % 8},
+            device_id={
+                "grp": (to_z // 4) * 4 + lane_x,
+                "gx": (to_z % 4) * 2 + (gx + dc) % 2,
+            },
             device_id_type=MESH,
         ).start()
 
-    seven = summed.at[pl.ds(0, 7)]
     pltpu.make_async_copy(seven, seven, gat_recv).wait()
     out = pltpu.make_async_copy(summed, grad_hbm, out_sem)
     out.start()
@@ -430,11 +477,18 @@
         scale_ref[k] = jnp.broadcast_to(value, (8, 128))
 
     out.wait()
-    sent = landed.at[pl.ds(0, 7)]
-    pltpu.make_async_copy(sent, sent, red_send).wait()
+    pltpu.make_async_copy(seven, seven, red_send).wait()
     pltpu.make_async_copy(seven, seven, gat_send).wait()
     pltpu.make_async_copy(some, some, s1_send).wait()
     pltpu.make_async_copy(few, few, s2_send).wait()
+    for dx, dy in order:
+
+        @pl.when(inside(dx, dy))
+        def _(dx=dx, dy=dy):
+            for copy in halo(dx, dy):
+                copy.wait_send()
+            if (dx, dy) in aux_order:
+                aux(dx, dy).wait_send()
 
 
 def body(
@@ -458,7 +512,7 @@
     grad, scale = pl.pallas_call(
         kernel,
         out_shape=(
-            jax.ShapeDtypeStruct((8, 4, 16, 128), F32),
+            jax.ShapeDtypeStruct((2, 4, 4, 16, 128), F32),
             jax.ShapeDtypeStruct((2, 8, 128), F32),
         ),
         in_specs=[hbm] * 6 + [pl.BlockSpec(memory_space=pltpu.SMEM)] + [hbm] * 3,
@@ -472,7 +526,7 @@
             pltpu.VMEM((16, 14, ROWS, 128), F32),
             pltpu.VMEM((2, 16, ROWS, 128), F32),
             pltpu.VMEM((8, 4, 16, 128), F32),
-            pltpu.VMEM((8, 4, 16, 128), F32),
+            pltpu.VMEM((2, 4, 4, 16, 128), F32),
             pltpu.VMEM((1, 128), F32),
             pltpu.VMEM((32, 128), F32),
             pltpu.VMEM((1, 128), F32),
@@ -482,8 +536,8 @@
             pltpu.SMEM((2,), jnp.int32),
             pltpu.VMEM((1, 128), jnp.int32),
             dma((9,)),
-            dma((8,)),
-            dma((8,)),
+            dma((32,)),
+            dma((32,)),
             dma,
             dma,
             dma,

time: 46.5 us -> 43.8 us (0.942)
  Pallas kernels: 45 us -> 42.3 us
    pallas_call x1, Pallas kernels: 45 us -> 42.3 us  [body(): pl.pallas_call(kernel, out_shape=(jax.ShapeDtypeStruct((2, 4, 4, 16, 128)...]
where the time goes in v3:
time: 43.8 us; the launch traced here: 43.7 us
  Pallas kernels  42.3 us (97%)
  other arithmetic  0.72 us (2%)
  between operations  0.67 us (2%)
    pallas_call x1, Pallas kernels, body(): pl.pallas_call(kernel, out_shape=(jax.ShapeDtypeStruct((2, 4, 4, 16, 128)...  42.3 us

profile of v3, /device:TPU:1, one launch (start us, length us, event | category | flops | bytes accessed | tf_op | source)
XLA Modules:
  0.0 43.7 jit_solution(7211339969020014230)
XLA Ops:
  0.7 42.3 %adjoint.1 = (f32[2,4,4,16,128]{4,3,2,1,0:T(8,128)S(1)}, f32[2,8,128]{2,1,0:T(8,128)S(1)}) custom-call(f32[1,3,16,16,128]{4,3,2,1,0:T(8,128)} %e_hbm.1, f32[1,3,16,16,128]{4,3,2,1,0:T(8,128)} %h_hbm.1, bf16[1,2,2,3,16,16,128]{6,5,4,3,2,1,0:T(8,128)(2,1)} %fwd_hbm.1, bf16[1,2,2,3,16,16,128]{6,5,4,3,2,1,0:T(8,128)(2,1)} %adj_hbm.1, f32[16,16,128]{2,1,0:T(8,128)} %perm_hbm.1, ...), custom_call_target="tpu_custom_call" | custom-call | tf_op jit(solution)/shard_map/adjoint/pallas_call | solution.py:512
  42.9 0.7 %broadcast_multiply_fusion = f32[2,16,16,128]{3,2,1,0:T(8,128)} fusion(f32[2,16,16,128]{3,2,1,0:T(8,128)S(1)} %bitcast.3, f32[2,128]{1,0:T(2,128)S(1)} %bitcast.4), kind=kLoop, calls=%fused_computation | loop fusion | flops 65536 | bytes 525312 | tf_op jit(solution)/shard_map/mul | solution.py:560
  (1 shorter events, 0.0 us)

commit v4 on v3

--- a/solution.py
+++ b/solution.py
@@ -72,6 +72,8 @@
     s2_send,
     s2_recv,
     out_sem,
+    round1,
+    round2,
 ):
     grp = lax.axis_index("grp")
     gx = lax.axis_index("gx")
@@ -80,19 +82,33 @@
     n_x = 8
     n_y = 8
 
+    lane_x = grp % 4
+    z_lo = gx // 2
+    core = gx % 2
+    place = z_hi * 4 + z_lo
     sides = [(dx, dy) for dx in (-1, 0, 1) for dy in (-1, 0, 1) if (dx, dy) != (0, 0)]
+
+    def device(x=0, y=0, z=0, c=0):
+        there = (place + z) % 8
+        return {
+            "grp": (there // 4) * 4 + (lane_x + x) % 4,
+            "gx": (there % 4) * 2 + (core + c) % 2,
+            "gy": (gy + y) % 8,
+        }
+
+    def tell(semaphore, **steps):
+        pl.semaphore_signal(
+            semaphore, inc=1, device_id=device(**steps), device_id_type=MESH
+        )
+
     barrier = pltpu.get_barrier_semaphore()
-
-    def greet(device):
-        pl.semaphore_signal(barrier, inc=1, device_id=device, device_id_type=MESH)
-
-    for dx, dy in sides:
-        device = {}
-        if dx != 0:
-            device["gx"] = (gx + dx) % n_x
-        if dy != 0:
-            device["gy"] = (gy + dy) % n_y
-        greet(device)
+    beyond = 2 * core - 1
+    for y in (-1, 1, 0):
+        tell(barrier, y=y, z=beyond, c=1)
+    for y in (-1, 1, 0):
+        tell(barrier, y=y, c=1)
+    for y in (-1, 1, -2, 2):
+        tell(barrier, y=y)
 
     own = (pl.ds(2, 16), pl.ds(2, 16))
     loads = [
@@ -109,13 +125,10 @@
     for i in (5, 2, 7, 0, 1, 6, 3, 4, 8):
         loads[i].start()
 
-    for d in range(4, 8):
-        greet({"grp": (grp + d) % 8})
-    for d in range(1, 4):
-        greet({"grp": (grp + d) % 8})
-    for d in range(2, 7):
-        greet({"gx": (gx + d) % 8})
-        greet({"gy": (gy + d) % 8})
+    for z in (-2, 2, -1, 1):
+        tell(barrier, z=z)
+    for x in (2, 1, 3):
+        tell(barrier, x=x)
 
     def inside(dx, dy):
         ok = None
@@ -125,7 +138,10 @@
                 ok = here if ok is None else jnp.logical_and(ok, here)
         return ok
 
-    pl.semaphore_wait(barrier, 25)
+    pl.semaphore_wait(barrier, 17)
+    for step in (-2, 2):
+        tell(round1, z=step)
+        tell(round1, y=step)
 
     def pick(d, wide):
         if d == 0:
@@ -259,6 +275,11 @@
 
     loop(0, 20, 4, make_damp)
 
+    pl.semaphore_wait(round1, 4)
+    for x in (2, 1, 3):
+        tell(round2, x=x)
+    tell(round2, c=1)
+
     loads[6].wait()
     row_id = lax.broadcasted_iota(jnp.int32, (8, 128), 0)
     tval = (row_id % 2 + 1).astype(F32)
@@ -311,6 +332,7 @@
     make_weights(0)
     make_weights(1)
 
+    pl.semaphore_wait(round2, 4)
     loads[0].wait()
     loads[1].wait()
 
@@ -362,7 +384,6 @@
     def read(first, p):
         return tuple(field[first + c, p] for c in range(3))
 
-    lane_x = grp % 4
     others = [(1, 2), (1, 1), (1, 3), (1, 0), (0, 2), (0, 1), (0, 3)]
 
     def peer(dz, dx):
@@ -447,7 +468,6 @@
     line = jnp.sum(rows1[...], axis=0, keepdims=True)
     row2[...] = line
     rows2[pl.ds(me2, 1), :] = line
-    place = me2 // 2
     steps = [(dz, dc) for dz in range(8) for dc in range(2) if (dz, dc) != (0, 0)]
     for dz, dc in sorted(steps, key=lambda d: -min(d[0], 8 - d[0])):
         to_z = (place + dz) % 8
@@ -547,6 +567,8 @@
             dma,
             dma,
             dma,
+            pltpu.SemaphoreType.REGULAR,
+            pltpu.SemaphoreType.REGULAR,
         ],
         compiler_params=pltpu.CompilerParams(
             collective_id=0, has_side_effects=True, vmem_limit_bytes=40 * 1024 * 1024

time: 43.8 us -> 42.4 us (0.968)
  Pallas kernels: 42.3 us -> 40.9 us
    pallas_call x1, Pallas kernels: 42.3 us -> 40.9 us  [body(): pl.pallas_call(kernel, out_shape=(jax.ShapeDtypeStruct((2, 4, 4, 16, 128)...]
where the time goes in v4:
time: 42.4 us; the launch traced here: 42.3 us
  Pallas kernels  40.9 us (96%)
  other arithmetic  0.72 us (2%)
  between operations  0.67 us (2%)
    pallas_call x1, Pallas kernels, body(): pl.pallas_call(kernel, out_shape=(jax.ShapeDtypeStruct((2, 4, 4, 16, 128)...  40.9 us

profile of v4, /device:TPU:1, one launch (start us, length us, event | category | flops | bytes accessed | tf_op | source)
XLA Modules:
  0.0 42.3 jit_solution(3254323397925315928)
XLA Ops:
  0.7 40.9 %adjoint.1 = (f32[2,4,4,16,128]{4,3,2,1,0:T(8,128)S(1)}, f32[2,8,128]{2,1,0:T(8,128)S(1)}) custom-call(f32[1,3,16,16,128]{4,3,2,1,0:T(8,128)} %e_hbm.1, f32[1,3,16,16,128]{4,3,2,1,0:T(8,128)} %h_hbm.1, bf16[1,2,2,3,16,16,128]{6,5,4,3,2,1,0:T(8,128)(2,1)} %fwd_hbm.1, bf16[1,2,2,3,16,16,128]{6,5,4,3,2,1,0:T(8,128)(2,1)} %adj_hbm.1, f32[16,16,128]{2,1,0:T(8,128)} %perm_hbm.1, ...), custom_call_target="tpu_custom_call" | custom-call | tf_op jit(solution)/shard_map/adjoint/pallas_call | solution.py:532
  41.5 0.7 %broadcast_multiply_fusion = f32[2,16,16,128]{3,2,1,0:T(8,128)} fusion(f32[2,16,16,128]{3,2,1,0:T(8,128)S(1)} %bitcast.3, f32[2,128]{1,0:T(2,128)S(1)} %bitcast.4), kind=kLoop, calls=%fused_computation | loop fusion | flops 65536 | bytes 525312 | tf_op jit(solution)/shard_map/mul | solution.py:582
  (1 shorter events, 0.0 us)

commit v5 on v4

--- a/solution.py
+++ b/solution.py
@@ -16,6 +16,7 @@
 
 PLANES = 21
 ROWS = 24
+READY = (7, 15)
 EX, EY, EZ, HX, HY, HZ, CO, DR = range(8)
 
 
@@ -41,7 +42,7 @@
     freq_hbm,
     pml_hbm,
     blocks_hbm,
-    grad_hbm,
+    grad_out,
     scale_ref,
     field,
     damp,
@@ -332,7 +333,6 @@
     make_weights(0)
     make_weights(1)
 
-    pl.semaphore_wait(round2, 4)
     loads[0].wait()
     loads[1].wait()
 
@@ -389,12 +389,12 @@
     def peer(dz, dx):
         return (z_hi + dz) % 2, (lane_x + dx) % 4
 
-    def send_quarter(q):
+    def send_planes(first, count):
         for dz, dx in others:
             k, j = peer(dz, dx)
             pltpu.make_async_remote_copy(
-                src_ref=term.at[k, 4 * q + j, pl.ds(2, 16), :],
-                dst_ref=landed.at[grp, q],
+                src_ref=term.at[k, j, pl.ds(first, count), pl.ds(2, 16), :],
+                dst_ref=landed.at[grp, pl.ds(first, count)],
                 send_sem=red_send,
                 recv_sem=red_recv,
                 device_id={"grp": k * 4 + j},
@@ -419,20 +419,22 @@
                 for c in range(3):
                     value = value + weights[x, k * 7 + 1 + c] * e1_last[c]
                     value = value + weights[x, k * 7 + 4 + c] * e2[c]
-                term[k, x] = value
-            if x % 4 == 3:
-                send_quarter(x // 4)
+                term[k, x % 4, x // 4] = value
+            if x == READY[0]:
+                pl.semaphore_wait(round2, 4)
+            if x in READY:
+                first = 0 if x == READY[0] else 1 + READY[READY.index(x) - 1] // 4
+                send_planes(first, x // 4 + 1 - first)
         e0 = e0_next
 
-    for q in range(4):
-        landed[grp, q] = term[z_hi, 4 * q + lane_x, 2:18, :]
+    landed[grp] = term[z_hi, lane_x, :, 2:18, :]
     seven = landed.at[pl.ds(0, 7)]
     pltpu.make_async_copy(seven, seven, red_recv).wait()
 
     total = landed[0]
     for j in range(1, 8):
         total = total + landed[j]
-    summed[z_hi, :, lane_x] = total
+    summed[...] = total
     square = jnp.sum(total * total, axis=0)
     line = jnp.sum(square, axis=0, keepdims=True)
 
@@ -451,11 +453,13 @@
             device_id_type=MESH,
         ).start()
 
-    mine = summed.at[z_hi, :, lane_x]
+    mine = grad_out.at[z_hi, :, lane_x]
+    out = pltpu.make_async_copy(summed, mine, out_sem)
+    out.start()
     for dz, dx in others:
         k, j = peer(dz, dx)
         pltpu.make_async_remote_copy(
-            src_ref=mine,
+            src_ref=summed,
             dst_ref=mine,
             send_sem=gat_send,
             recv_sem=gat_recv,
@@ -483,9 +487,20 @@
             device_id_type=MESH,
         ).start()
 
+    for dx, dy in order:
+
+        @pl.when(inside(dx, dy))
+        def _(dx=dx, dy=dy):
+            for copy in halo(dx, dy):
+                copy.wait_send()
+            if (dx, dy) in aux_order:
+                aux(dx, dy).wait_send()
+
+    pltpu.make_async_copy(seven, seven, red_send).wait()
+    pltpu.make_async_copy(seven, seven, gat_send).wait()
+    pltpu.make_async_copy(some, some, s1_send).wait()
+    out.wait()
     pltpu.make_async_copy(seven, seven, gat_recv).wait()
-    out = pltpu.make_async_copy(summed, grad_hbm, out_sem)
-    out.start()
 
     few = rows2.at[pl.ds(0, 15)]
     pltpu.make_async_copy(few, few, s2_recv).wait()
@@ -495,20 +510,7 @@
         squares = jnp.sum(squares, axis=1, keepdims=True)
         value = lax.rsqrt(squares / count + 1e-05)
         scale_ref[k] = jnp.broadcast_to(value, (8, 128))
-
-    out.wait()
-    pltpu.make_async_copy(seven, seven, red_send).wait()
-    pltpu.make_async_copy(seven, seven, gat_send).wait()
-    pltpu.make_async_copy(some, some, s1_send).wait()
     pltpu.make_async_copy(few, few, s2_send).wait()
-    for dx, dy in order:
-
-        @pl.when(inside(dx, dy))
-        def _(dx=dx, dy=dy):
-            for copy in halo(dx, dy):
-                copy.wait_send()
-            if (dx, dy) in aux_order:
-                aux(dx, dy).wait_send()
 
 
 def body(
@@ -544,9 +546,9 @@
             pltpu.VMEM((2, 2, 3, 16, 16, 128), jnp.bfloat16),
             pltpu.VMEM((16, 128), F32),
             pltpu.VMEM((16, 14, ROWS, 128), F32),
-            pltpu.VMEM((2, 16, ROWS, 128), F32),
+            pltpu.VMEM((2, 4, 4, ROWS, 128), F32),
             pltpu.VMEM((8, 4, 16, 128), F32),
-            pltpu.VMEM((2, 4, 4, 16, 128), F32),
+            pltpu.VMEM((4, 16, 128), F32),
             pltpu.VMEM((1, 128), F32),
             pltpu.VMEM((32, 128), F32),
             pltpu.VMEM((1, 128), F32),

time: 42.4 us -> 42 us (level)
  no operation moved by 1% of the time
where the time goes in v5:
time: 42 us; the launch traced here: 41.9 us
  Pallas kernels  40.5 us (96%)
  other arithmetic  0.72 us (2%)
  between operations  0.67 us (2%)
    pallas_call x1, Pallas kernels, body(): pl.pallas_call(kernel, out_shape=(jax.ShapeDtypeStruct((2, 4, 4, 16, 128)...  40.5 us

profile of v5, /device:TPU:1, one launch (start us, length us, event | category | flops | bytes accessed | tf_op | source)
XLA Modules:
  0.0 41.9 jit_solution(1181577777860855083)
XLA Ops:
  0.7 40.5 %adjoint.1 = (f32[2,4,4,16,128]{4,3,2,1,0:T(8,128)S(1)}, f32[2,8,128]{2,1,0:T(8,128)S(1)}) custom-call(f32[1,3,16,16,128]{4,3,2,1,0:T(8,128)} %e_hbm.1, f32[1,3,16,16,128]{4,3,2,1,0:T(8,128)} %h_hbm.1, bf16[1,2,2,3,16,16,128]{6,5,4,3,2,1,0:T(8,128)(2,1)} %fwd_hbm.1, bf16[1,2,2,3,16,16,128]{6,5,4,3,2,1,0:T(8,128)(2,1)} %adj_hbm.1, f32[16,16,128]{2,1,0:T(8,128)} %perm_hbm.1, ...), custom_call_target="tpu_custom_call" | custom-call | tf_op jit(solution)/shard_map/adjoint/pallas_call | solution.py:534
  41.1 0.7 %broadcast_multiply_fusion = f32[2,16,16,128]{3,2,1,0:T(8,128)} fusion(f32[2,16,16,128]{3,2,1,0:T(8,128)S(1)} %bitcast.3, f32[2,128]{1,0:T(2,128)S(1)} %bitcast.4), kind=kLoop, calls=%fused_computation | loop fusion | flops 65536 | bytes 525312 | tf_op jit(solution)/shard_map/mul | solution.py:584
  (1 shorter events, 0.0 us)

commit v6 on v5

--- a/solution.py
+++ b/solution.py
@@ -438,18 +438,18 @@
     square = jnp.sum(total * total, axis=0)
     line = jnp.sum(square, axis=0, keepdims=True)
 
-    me1 = lane_x * 8 + gy
-    me2 = z_hi * 8 + gx
+    me1 = gy * 2 + core
+    me2 = place * 4 + lane_x
     row1[...] = line
     rows1[pl.ds(me1, 1), :] = line
-    steps = [(dx, dy) for dx in range(4) for dy in range(8) if (dx, dy) != (0, 0)]
-    for dx, dy in sorted(steps, key=lambda d: -min(d[0], 4 - d[0]) - min(d[1], 8 - d[1])):
+    steps = [(dy, dc) for dy in range(8) for dc in range(2) if (dy, dc) != (0, 0)]
+    for dy, dc in sorted(steps, key=lambda d: -min(d[0], 8 - d[0])):
         pltpu.make_async_remote_copy(
             src_ref=row1,
             dst_ref=rows1.at[pl.ds(me1, 1)],
             send_sem=s1_send,
             recv_sem=s1_recv,
-            device_id={"grp": z_hi * 4 + (lane_x + dx) % 4, "gy": (gy + dy) % 8},
+            device_id=device(y=dy, c=dc),
             device_id_type=MESH,
         ).start()
 
@@ -467,23 +467,19 @@
             device_id_type=MESH,
         ).start()
 
-    some = rows1.at[pl.ds(0, 31)]
+    some = rows1.at[pl.ds(0, 15)]
     pltpu.make_async_copy(some, some, s1_recv).wait()
     line = jnp.sum(rows1[...], axis=0, keepdims=True)
     row2[...] = line
     rows2[pl.ds(me2, 1), :] = line
-    steps = [(dz, dc) for dz in range(8) for dc in range(2) if (dz, dc) != (0, 0)]
-    for dz, dc in sorted(steps, key=lambda d: -min(d[0], 8 - d[0])):
-        to_z = (place + dz) % 8
+    steps = [(dz, dx) for dz in range(8) for dx in range(4) if (dz, dx) != (0, 0)]
+    for dz, dx in sorted(steps, key=lambda d: -min(d[0], 8 - d[0]) - min(d[1], 4 - d[1])):
         pltpu.make_async_remote_copy(
             src_ref=row2,
             dst_ref=rows2.at[pl.ds(me2, 1)],
             send_sem=s2_send,
             recv_sem=s2_recv,
-            device_id={
-                "grp": (to_z // 4) * 4 + lane_x,
-                "gx": (to_z % 4) * 2 + (gx + dc) % 2,
-            },
+            device_id=device(z=dz, x=dx),
             device_id_type=MESH,
         ).start()
 
@@ -502,11 +498,11 @@
     out.wait()
     pltpu.make_async_copy(seven, seven, gat_recv).wait()
 
-    few = rows2.at[pl.ds(0, 15)]
+    few = rows2.at[pl.ds(0, 31)]
     pltpu.make_async_copy(few, few, s2_recv).wait()
     count = float(128 * BS * BS * 128)
     for k in range(2):
-        squares = jnp.sum(rows2[8 * k : 8 * k + 8], axis=0, keepdims=True)
+        squares = jnp.sum(rows2[16 * k : 16 * k + 16], axis=0, keepdims=True)
         squares = jnp.sum(squares, axis=1, keepdims=True)
         value = lax.rsqrt(squares / count + 1e-05)
         scale_ref[k] = jnp.broadcast_to(value, (8, 128))
@@ -550,9 +546,9 @@
             pltpu.VMEM((8, 4, 16, 128), F32),
             pltpu.VMEM((4, 16, 128), F32),
             pltpu.VMEM((1, 128), F32),
+            pltpu.VMEM((16, 128), F32),
+            pltpu.VMEM((1, 128), F32),
             pltpu.VMEM((32, 128), F32),
-            pltpu.VMEM((1, 128), F32),
-            pltpu.VMEM((16, 128), F32),
             pltpu.VMEM((1, 16, 16), F32),
             pltpu.SMEM((1, 2), F32),
             pltpu.SMEM((2,), jnp.int32),

time: 42 us -> 41.5 us (0.988)
  Pallas kernels: 40.5 us -> 40 us
    pallas_call x1, Pallas kernels: 40.5 us -> 40 us  [body(): pl.pallas_call(kernel, out_shape=(jax.ShapeDtypeStruct((2, 4, 4, 16, 128)...]
where the time goes in v6:
time: 41.5 us; the launch traced here: 41.4 us
  Pallas kernels  40 us (96%)
  other arithmetic  0.72 us (2%)
  between operations  0.67 us (2%)
    pallas_call x1, Pallas kernels, body(): pl.pallas_call(kernel, out_shape=(jax.ShapeDtypeStruct((2, 4, 4, 16, 128)...  40 us

profile of v6, /device:TPU:1, one launch (start us, length us, event | category | flops | bytes accessed | tf_op | source)
XLA Modules:
  0.0 41.4 jit_solution(2949825226273407068)
XLA Ops:
  0.7 40.0 %adjoint.1 = (f32[2,4,4,16,128]{4,3,2,1,0:T(8,128)S(1)}, f32[2,8,128]{2,1,0:T(8,128)S(1)}) custom-call(f32[1,3,16,16,128]{4,3,2,1,0:T(8,128)} %e_hbm.1, f32[1,3,16,16,128]{4,3,2,1,0:T(8,128)} %h_hbm.1, bf16[1,2,2,3,16,16,128]{6,5,4,3,2,1,0:T(8,128)(2,1)} %fwd_hbm.1, bf16[1,2,2,3,16,16,128]{6,5,4,3,2,1,0:T(8,128)(2,1)} %adj_hbm.1, f32[16,16,128]{2,1,0:T(8,128)} %perm_hbm.1, ...), custom_call_target="tpu_custom_call" | custom-call | tf_op jit(solution)/shard_map/adjoint/pallas_call | solution.py:530
  40.7 0.7 %broadcast_multiply_fusion = f32[2,16,16,128]{3,2,1,0:T(8,128)} fusion(f32[2,16,16,128]{3,2,1,0:T(8,128)S(1)} %bitcast.3, f32[2,128]{1,0:T(2,128)S(1)} %bitcast.4), kind=kLoop, calls=%fused_computation | loop fusion | flops 65536 | bytes 525312 | tf_op jit(solution)/shard_map/mul | solution.py:580
  (1 shorter events, 0.0 us)

commit v7 on v6

--- a/solution.py
+++ b/solution.py
@@ -438,18 +438,18 @@
     square = jnp.sum(total * total, axis=0)
     line = jnp.sum(square, axis=0, keepdims=True)
 
-    me1 = gy * 2 + core
-    me2 = place * 4 + lane_x
+    me1 = place * 2 + core
+    me2 = gy * 4 + lane_x
     row1[...] = line
     rows1[pl.ds(me1, 1), :] = line
-    steps = [(dy, dc) for dy in range(8) for dc in range(2) if (dy, dc) != (0, 0)]
-    for dy, dc in sorted(steps, key=lambda d: -min(d[0], 8 - d[0])):
+    steps = [(dz, dc) for dz in range(8) for dc in range(2) if (dz, dc) != (0, 0)]
+    for dz, dc in sorted(steps, key=lambda d: -min(d[0], 8 - d[0])):
         pltpu.make_async_remote_copy(
             src_ref=row1,
             dst_ref=rows1.at[pl.ds(me1, 1)],
             send_sem=s1_send,
             recv_sem=s1_recv,
-            device_id=device(y=dy, c=dc),
+            device_id=device(z=dz, c=dc),
             device_id_type=MESH,
         ).start()
 
@@ -469,17 +469,18 @@
 
     some = rows1.at[pl.ds(0, 15)]
     pltpu.make_async_copy(some, some, s1_recv).wait()
-    line = jnp.sum(rows1[...], axis=0, keepdims=True)
-    row2[...] = line
-    rows2[pl.ds(me2, 1), :] = line
-    steps = [(dz, dx) for dz in range(8) for dx in range(4) if (dz, dx) != (0, 0)]
-    for dz, dx in sorted(steps, key=lambda d: -min(d[0], 8 - d[0]) - min(d[1], 4 - d[1])):
+    for k in range(2):
+        line = jnp.sum(rows1[8 * k : 8 * k + 8], axis=0, keepdims=True)
+        row2[k] = line
+        rows2[k, pl.ds(me2, 1), :] = line
+    steps = [(dy, dx) for dy in range(8) for dx in range(4) if (dy, dx) != (0, 0)]
+    for dy, dx in sorted(steps, key=lambda d: -min(d[0], 8 - d[0]) - min(d[1], 4 - d[1])):
         pltpu.make_async_remote_copy(
             src_ref=row2,
-            dst_ref=rows2.at[pl.ds(me2, 1)],
+            dst_ref=rows2.at[:, pl.ds(me2, 1)],
             send_sem=s2_send,
             recv_sem=s2_recv,
-            device_id=device(z=dz, x=dx),
+            device_id=device(y=dy, x=dx),
             device_id_type=MESH,
         ).start()
 
@@ -498,11 +499,11 @@
     out.wait()
     pltpu.make_async_copy(seven, seven, gat_recv).wait()
 
-    few = rows2.at[pl.ds(0, 31)]
+    few = rows2.at[:, pl.ds(0, 31)]
     pltpu.make_async_copy(few, few, s2_recv).wait()
     count = float(128 * BS * BS * 128)
     for k in range(2):
-        squares = jnp.sum(rows2[16 * k : 16 * k + 16], axis=0, keepdims=True)
+        squares = jnp.sum(rows2[k], axis=0, keepdims=True)
         squares = jnp.sum(squares, axis=1, keepdims=True)
         value = lax.rsqrt(squares / count + 1e-05)
         scale_ref[k] = jnp.broadcast_to(value, (8, 128))
@@ -547,8 +548,8 @@
             pltpu.VMEM((4, 16, 128), F32),
             pltpu.VMEM((1, 128), F32),
             pltpu.VMEM((16, 128), F32),
-            pltpu.VMEM((1, 128), F32),
-            pltpu.VMEM((32, 128), F32),
+            pltpu.VMEM((2, 1, 128), F32),
+            pltpu.VMEM((2, 32, 128), F32),
             pltpu.VMEM((1, 16, 16), F32),
             pltpu.SMEM((1, 2), F32),
             pltpu.SMEM((2,), jnp.int32),

time: 41.5 us -> 41.7 us (level)
  no operation moved by 1% of the time
where the time goes in v7:
time: 41.7 us; the launch traced here: 41.6 us
  Pallas kernels  40.2 us (96%)
  other arithmetic  0.72 us (2%)
  between operations  0.67 us (2%)
    pallas_call x1, Pallas kernels, body(): pl.pallas_call(kernel, out_shape=(jax.ShapeDtypeStruct((2, 4, 4, 16, 128)...  40.2 us

profile of v7, /device:TPU:1, one launch (start us, length us, event | category | flops | bytes accessed | tf_op | source)
XLA Modules:
  0.0 41.6 jit_solution(591440804281462839)
XLA Ops:
  0.7 40.2 %adjoint.1 = (f32[2,4,4,16,128]{4,3,2,1,0:T(8,128)S(1)}, f32[2,8,128]{2,1,0:T(8,128)S(1)}) custom-call(f32[1,3,16,16,128]{4,3,2,1,0:T(8,128)} %e_hbm.1, f32[1,3,16,16,128]{4,3,2,1,0:T(8,128)} %h_hbm.1, bf16[1,2,2,3,16,16,128]{6,5,4,3,2,1,0:T(8,128)(2,1)} %fwd_hbm.1, bf16[1,2,2,3,16,16,128]{6,5,4,3,2,1,0:T(8,128)(2,1)} %adj_hbm.1, f32[16,16,128]{2,1,0:T(8,128)} %perm_hbm.1, ...), custom_call_target="tpu_custom_call" | custom-call | tf_op jit(solution)/shard_map/adjoint/pallas_call | solution.py:531
  40.8 0.7 %broadcast_multiply_fusion = f32[2,16,16,128]{3,2,1,0:T(8,128)} fusion(f32[2,16,16,128]{3,2,1,0:T(8,128)S(1)} %bitcast.3, f32[2,128]{1,0:T(2,128)S(1)} %bitcast.4), kind=kLoop, calls=%fused_computation | loop fusion | flops 65536 | bytes 525312 | tf_op jit(solution)/shard_map/mul | solution.py:581
  (1 shorter events, 0.0 us)
